TPU v7x, 512 devices: a whole 4x4x16 slice. The times are simulated.
512 devices in a mesh: lon: 32 (over y, z_lo, core), lat: 16 (over x, z_hi).
Axes of the slice: x: 4, y: 4, z: 16 (z_hi: 4, z_lo: 4; z = z_hi * 4 + z_lo), core: 2. Of those that a mesh axis runs over, the one named last changes fastest.
Arguments:
- velocity: float32 [2, 768, 4096], P(None, 'lat', 'lon'), may hold values from -6 to 6
- stress: float32 [3, 768, 4096], P(None, 'lat', 'lon'), may hold values from -6 to 6
- strength: float32 [768, 4096], P('lat', 'lon'), may hold values from 0.3 to 3
- wind_stress: bfloat16 [2, 768, 4096], P(None, 'lat', 'lon'), may hold values from -6 to 6
- ice_mask: int32 [768, 4096], P('lat', 'lon'), may hold values from 0 to 1, as said below
- start_step: int32 [1], replicated, may hold values from 0 to 114
- velocity_cotangent: float32 [2, 768, 4096], P(None, 'lat', 'lon'), may hold values from -6 to 6
Outputs:
- final_velocity: float32 [2, 768, 4096], P(None, 'lat', 'lon')
- velocity_gradient: float32 [2, 768, 4096], P(None, 'lat', 'lon')
- stress_gradient: float32 [3, 768, 4096], P(None, 'lat', 'lon')
Inputs may be any that keep to these rules, and one draw needn't show every extreme that they name: `ice_mask`: 0 or 1 in every cell.
All inputs are finite; a program needn't handle non-finite values.
Results may differ from a plain program's by a relative error of at most 0.00045.
Values sent between devices are 32-bit elements; how exact they have to be, the bound alone decides.
A program may use at most 64 MiB of HBM per device.

v0:
```python
from functools import partial

import jax
import jax.numpy as jnp
from jax import lax
from jax.sharding import PartitionSpec as P

NSUB = 6
EVP_TOTAL = 120


relax_rate = 0.5
step_factor = 0.5
drag_rate = 1.0
ellipse_sq = 4.0
delta_min_sq = 0.25


def extended_2(cells, sides, width, closed):
    for axis, dim in sides:
        count = lax.axis_size(axis)
        ends = count if closed else count - 1
        head = lax.slice_in_dim(cells, 0, width, axis=dim)
        tail = lax.slice_in_dim(cells, cells.shape[dim] - width, cells.shape[dim], axis=dim)
        cells = jnp.concatenate(
            [
                lax.ppermute(tail, axis, [(i, (i + 1) % count) for i in range(ends)]),
                cells,
                lax.ppermute(head, axis, [((i + 1) % count, i) for i in range(ends)]),
            ],
            axis=dim,
        )
    return cells


def stress_update(stress_old, vel_west, vel_east, vel_south, vel_north, strength, ice_cover):
    strain_xx = 0.5 * (vel_east[0] - vel_west[0])
    strain_yy = 0.5 * (vel_north[1] - vel_south[1])
    shear_rate = 0.5 * (vel_north[0] - vel_south[0]) + 0.5 * (vel_east[1] - vel_west[1])
    divergence = strain_xx + strain_yy
    tension = strain_xx - strain_yy
    delta_norm = jnp.sqrt(
        divergence * divergence
        + (tension * tension + shear_rate * shear_rate) / ellipse_sq
        + delta_min_sq
    )
    viscous_ratio = strength / delta_norm
    target = jnp.stack(
        [
            viscous_ratio * divergence - strength,
            viscous_ratio * tension / ellipse_sq,
            0.5 * viscous_ratio * shear_rate / ellipse_sq,
        ]
    )
    return (stress_old + relax_rate * target) / (1.0 + relax_rate) * ice_cover


def velocity_update(
    velocity,
    xx_west,
    xx_east,
    xy_west,
    xy_east,
    yy_south,
    yy_north,
    xy_south,
    xy_north,
    wind_force,
    weight,
    coriolis,
    ice_cover,
):
    force_x = 0.5 * (xx_east - xx_west) + 0.5 * (xy_north - xy_south)
    force_y = 0.5 * (xy_east - xy_west) + 0.5 * (yy_north - yy_south)
    right_u = velocity[0] + step_factor * (force_x + weight * wind_force[0])
    right_v = velocity[1] + step_factor * (force_y + weight * wind_force[1])
    diag_term = 1.0 + step_factor * drag_rate
    turn_term = step_factor * coriolis
    det_term = diag_term * diag_term + turn_term * turn_term
    return (
        jnp.stack(
            [
                (diag_term * right_u + turn_term * right_v) / det_term,
                (diag_term * right_v - turn_term * right_u) / det_term,
            ]
        )
        * ice_cover
    )


def shift_lon(stack_in, west_side, east_side):
    from_west = jnp.concatenate([west_side[:, :, None], stack_in[:, :, :-1]], axis=2)
    from_east = jnp.concatenate([stack_in[:, :, 1:], east_side[:, :, None]], axis=2)
    return (from_west, from_east)


def shift_lat(stack_in, south_side, north_side):
    from_south = jnp.concatenate([south_side[:, None, :], stack_in[:, :-1, :]], axis=1)
    from_north = jnp.concatenate([stack_in[:, 1:, :], north_side[:, None, :]], axis=1)
    return (from_south, from_north)


def edge_pair(values):
    return (
        jnp.stack([values[:, :, 0], values[:, :, -1]], axis=1),
        jnp.stack([values[:, 0, :], values[:, -1, :]], axis=1),
    )


def velocity_edges(velocity):
    return edge_pair(velocity)


def stress_edges(stress_new):
    return edge_pair(stress_new)


def stress_local(stress_old, velocity, lon_edges, lat_edges, strength, ice_cover):
    vel_west, vel_east = shift_lon(velocity, lon_edges[0], lon_edges[1])
    vel_south, vel_north = shift_lat(velocity, lat_edges[0], lat_edges[1])
    return stress_update(stress_old, vel_west, vel_east, vel_south, vel_north, strength, ice_cover)


def velocity_local(
    velocity, stress_new, lon_edges, lat_edges, wind_force, weight, coriolis, ice_cover
):
    west_side, east_side = lon_edges
    south_side, north_side = lat_edges
    west_side = jnp.stack([0.5 * (west_side[0] + west_side[1]), west_side[2]])
    east_side = jnp.stack([0.5 * (east_side[0] + east_side[1]), east_side[2]])
    south_side = jnp.stack([0.5 * (south_side[0] - south_side[1]), south_side[2]])
    north_side = jnp.stack([0.5 * (north_side[0] - north_side[1]), north_side[2]])
    lon_own = jnp.stack([0.5 * (stress_new[0] + stress_new[1]), stress_new[2]])
    lat_own = jnp.stack([0.5 * (stress_new[0] - stress_new[1]), stress_new[2]])
    from_west, from_east = shift_lon(lon_own, west_side, east_side)
    from_south, from_north = shift_lat(lat_own, south_side, north_side)
    return velocity_update(
        velocity,
        from_west[0],
        from_east[0],
        from_west[1],
        from_east[1],
        from_south[0],
        from_north[0],
        from_south[1],
        from_north[1],
        wind_force,
        weight,
        coriolis,
        ice_cover,
    )


def lon_rims(edge_pack):
    extended = extended_2(edge_pack, (("lon", 1),), 1, True)
    return (extended[:, 0], extended[:, 3])


def lat_rims(edge_pack):
    extended = extended_2(edge_pack, (("lat", 1),), 1, False)
    return (extended[:, 0], extended[:, 3])


def reverse_sources(received):
    return lax.all_to_all(jnp.flip(received, 1), "lon", split_axis=1, concat_axis=1, tiled=True)


def mirror(edge_row):
    columns = edge_row.shape[1]
    piece_count = lax.axis_size("lon")
    pieces = edge_row.reshape(edge_row.shape[0], piece_count, columns // piece_count)
    moved_row = reverse_sources(
        lax.all_to_all(pieces, "lon", split_axis=1, concat_axis=1, tiled=True)
    ).reshape(edge_row.shape)
    return jnp.flip(moved_row, 1)


def across(lon_pack, lat_pack, fold_sign, top_band):
    west_side, east_side = lon_rims(lon_pack)
    south_side, north_side = lat_rims(lat_pack)
    folded = fold_sign * mirror(lat_pack[:, 1])
    north_side = jnp.where(top_band, folded, north_side)
    return ((west_side, east_side), (south_side, north_side))


def across_back(lon_grads, lat_grads, fold_sign, top_band):
    back_west, back_east = lon_rims(jnp.stack([lon_grads[0], lon_grads[1]], axis=1))
    north_grad = lat_grads[1]
    zero_row = jnp.zeros_like(north_grad)
    sent_north = jnp.where(top_band, zero_row, north_grad)
    back_south, back_north = lat_rims(jnp.stack([lat_grads[0], sent_north], axis=1))
    folded = fold_sign * mirror(jnp.where(top_band, north_grad, zero_row))
    back_north = back_north + jnp.where(top_band, folded, zero_row)
    return (jnp.stack([back_west, back_east], axis=1), jnp.stack([back_south, back_north], axis=1))


def shards(velocity, stress, strength, wind_stress, ice_mask, start_step, velocity_cotangent):
    ice_cover = ice_mask.astype(jnp.float32)
    wind_force = wind_stress.astype(jnp.float32)
    lat_rows = velocity.shape[1]
    band_index = lax.axis_index("lat")
    band_count = lax.axis_size("lat")
    top_band = band_index == band_count - 1
    global_rows = (band_index * lat_rows + jnp.arange(lat_rows, dtype=jnp.int32)).astype(
        jnp.float32
    )
    coriolis = (1.2 * ((2.0 * global_rows + 1.0) / (lat_rows * band_count) - 1.0))[:, None]
    start_value = start_step[0].astype(jnp.float32)
    saved_steps = []
    vel_now, stress_now = (velocity, stress)
    for step_index in range(NSUB):
        weight = (start_value + (step_index + 1)) / EVP_TOTAL
        vel_pack_lon, vel_pack_lat = velocity_edges(vel_now)
        vel_lon, vel_lat = across(vel_pack_lon, vel_pack_lat, -1.0, top_band)
        stress_new = stress_local(stress_now, vel_now, vel_lon, vel_lat, strength, ice_cover)
        str_pack_lon, str_pack_lat = stress_edges(stress_new)
        str_lon, str_lat = across(str_pack_lon, str_pack_lat, 1.0, top_band)
        vel_new = velocity_local(
            vel_now, stress_new, str_lon, str_lat, wind_force, weight, coriolis, ice_cover
        )
        saved_steps.append(
            (vel_now, stress_now, vel_lon, vel_lat, stress_new, str_lon, str_lat, weight)
        )
        vel_now, stress_now = (vel_new, stress_new)
    vel_grad = velocity_cotangent
    stress_grad = jnp.zeros_like(stress)
    for step_index in reversed(range(NSUB)):
        vel_old, stress_old, vel_lon, vel_lat, stress_new, str_lon, str_lat, weight = saved_steps[
            step_index
        ]
        velocity_stepper = partial(
            velocity_local,
            wind_force=wind_force,
            weight=weight,
            coriolis=coriolis,
            ice_cover=ice_cover,
        )
        _, pull_velocity = jax.vjp(velocity_stepper, vel_old, stress_new, str_lon, str_lat)
        grad_vel_direct, grad_stress_new, grad_str_lon, grad_str_lat = pull_velocity(vel_grad)
        back_lon, back_lat = across_back(grad_str_lon, grad_str_lat, 1.0, top_band)
        _, pull_stress_edges = jax.vjp(stress_edges, stress_new)
        grad_stress_new = grad_stress_new + pull_stress_edges((back_lon, back_lat))[0] + stress_grad
        stress_stepper = partial(stress_local, strength=strength, ice_cover=ice_cover)
        _, pull_stress = jax.vjp(stress_stepper, stress_old, vel_old, vel_lon, vel_lat)
        stress_grad, grad_vel_strain, grad_vel_lon, grad_vel_lat = pull_stress(grad_stress_new)
        back_lon, back_lat = across_back(grad_vel_lon, grad_vel_lat, -1.0, top_band)
        _, pull_vel_edges = jax.vjp(velocity_edges, vel_old)
        vel_grad = grad_vel_direct + grad_vel_strain + pull_vel_edges((back_lon, back_lat))[0]
    return (vel_now, vel_grad, stress_grad)


def solution(mesh):
    placed = (
        P(None, "lat", "lon"),
        P(None, "lat", "lon"),
        P("lat", "lon"),
        P(None, "lat", "lon"),
        P("lat", "lon"),
        P(),
        P(None, "lat", "lon"),
    )
    return jax.shard_map(
        shards,
        mesh=mesh,
        in_specs=placed,
        out_specs=(P(None, "lat", "lon"), P(None, "lat", "lon"), P(None, "lat", "lon")),
        check_vma=False,
    )
```

profile of v0, /device:TPU:6, one launch (start us, length us, event | category | flops | bytes accessed | tf_op | source)
XLA Modules:
  0.0 989.8 jit_solution(9389736972631949596)
XLA Ops:
  2.1 9.1 all-to-all-start
  11.2 10.3 %collective-permute-start.2 = (f32[2,1,128]{2,0,1:T(2,128)S(1)}, f32[2,1,128]{2,0,1:T(2,128)S(1)}, u32[]{:S(2)}, u32[]{:S(2)}) collective-permute-start(f32[2,1,128]{2,0,1:T(2,128)S(1)} %bitcast.1176), channel_id=1, source_target_pairs={{1,0},{2,1},{3,2},{4,3},{5,4},{6,5},{7,6},{8,7},{9,8},{10,9},{11,1... | collective-permute-start | bytes 3080 | tf_op jit(solution)/shard_map/ppermute | solution.py:29
  55.9 8.4 collective-permute-start.6
  68.3 7.5 collective-permute-start.4
  85.5 7.9 all-to-all-done.3
  98.6 8.7 collective-permute-start.10
  169.7 7.9 all-to-all-done.7
  227.3 7.8 collective-permute-start.23
  248.8 7.9 all-to-all-done.11
  328.0 7.9 all-to-all-done.15
  409.1 7.9 all-to-all-done.19
  479.5 7.7 all-to-all-start.25
  487.4 7.8 all-to-all-done.25
  535.2 7.7 all-to-all-start.28
  554.7 7.5 collective-permute-start.58
  567.2 7.7 all-to-all-done.29
  612.9 7.7 all-to-all-start.32
  647.6 7.7 all-to-all-done.33
  719.8 7.7 all-to-all-start.37
  727.7 7.8 all-to-all-done.37
  809.9 7.7 all-to-all-done.41
  859.3 7.7 all-to-all-start.44
  868.9 7.8 collective-permute-start.89
  894.0 7.6 all-to-all-done.45
  (889 shorter events, 792.3 us)
Async XLA Ops:
  11.2 38.3 %collective-permute-start.2 = (f32[2,1,128]{2,0,1:T(2,128)S(1)}, f32[2,1,128]{2,0,1:T(2,128)S(1)}, u32[]{:S(2)}, u32[]{:S(2)}) collective-permute-start(f32[2,1,128]{2,0,1:T(2,128)S(1)} %bitcast.1176), channel_id=1, source_target_pairs={{1,0},{2,1},{3,2},{4,3},{5,4},{6,5},{7,6},{8,7},{9,8},{10,9},{11,1... | collective-permute-start | bytes 3080 | tf_op jit(solution)/shard_map/ppermute | solution.py:29
  55.9 37.7 %collective-permute-start.6 = (f32[3,1,128]{2,0,1:T(4,128)S(1)}, f32[3,1,128]{2,0,1:T(4,128)S(1)}, u32[]{:S(2)}, u32[]{:S(2)}) collective-permute-start(f32[3,1,128]{2,0,1:T(4,128)S(1)} %copy.3968), channel_id=1, source_target_pairs={{1,0},{2,1},{3,2},{4,3},{5,4},{6,5},{7,6},{8,7},{9,8},{10,9},{11,1... | collective-permute-start | bytes 4616 | tf_op jit(solution)/shard_map/ppermute | solution.py:29
  98.6 33.8 %collective-permute-start.10 = (f32[2,1,128]{2,0,1:T(2,128)S(1)}, f32[2,1,128]{2,0,1:T(2,128)S(1)}, u32[]{:S(2)}, u32[]{:S(2)}) collective-permute-start(f32[2,1,128]{2,0,1:T(2,128)S(1)} %bitcast.1181), channel_id=1, source_target_pairs={{1,0},{2,1},{3,2},{4,3},{5,4},{6,5},{7,6},{8,7},{9,8},{10,9},{11,1... | collective-permute-start | bytes 3080 | tf_op jit(solution)/shard_map/ppermute | solution.py:29
  146.2 31.6 %collective-permute-start.14 = (f32[3,1,128]{2,0,1:T(4,128)S(1)}, f32[3,1,128]{2,0,1:T(4,128)S(1)}, u32[]{:S(2)}, u32[]{:S(2)}) collective-permute-start(f32[3,1,128]{2,0,1:T(4,128)S(1)} %copy.3970), channel_id=1, source_target_pairs={{1,0},{2,1},{3,2},{4,3},{5,4},{6,5},{7,6},{8,7},{9,8},{10,9},{11,1... | collective-permute-start | bytes 4616 | tf_op jit(solution)/shard_map/ppermute | solution.py:29
  225.3 31.6 %collective-permute-start.22 = (f32[3,1,128]{2,0,1:T(4,128)S(1)}, f32[3,1,128]{2,0,1:T(4,128)S(1)}, u32[]{:S(2)}, u32[]{:S(2)}) collective-permute-start(f32[3,1,128]{2,0,1:T(4,128)S(1)} %copy.3972), channel_id=1, source_target_pairs={{1,0},{2,1},{3,2},{4,3},{5,4},{6,5},{7,6},{8,7},{9,8},{10,9},{11,1... | collective-permute-start | bytes 4616 | tf_op jit(solution)/shard_map/ppermute | solution.py:29
  304.5 31.6 %collective-permute-start.30 = (f32[3,1,128]{2,0,1:T(4,128)S(1)}, f32[3,1,128]{2,0,1:T(4,128)S(1)}, u32[]{:S(2)}, u32[]{:S(2)}) collective-permute-start(f32[3,1,128]{2,0,1:T(4,128)S(1)} %copy.3974), channel_id=1, source_target_pairs={{1,0},{2,1},{3,2},{4,3},{5,4},{6,5},{7,6},{8,7},{9,8},{10,9},{11,1... | collective-permute-start | bytes 4616 | tf_op jit(solution)/shard_map/ppermute | solution.py:29
  385.6 31.6 %collective-permute-start.38 = (f32[3,1,128]{2,0,1:T(4,128)S(1)}, f32[3,1,128]{2,0,1:T(4,128)S(1)}, u32[]{:S(2)}, u32[]{:S(2)}) collective-permute-start(f32[3,1,128]{2,0,1:T(4,128)S(1)} %copy.3976), channel_id=1, source_target_pairs={{1,0},{2,1},{3,2},{4,3},{5,4},{6,5},{7,6},{8,7},{9,8},{10,9},{11,1... | collective-permute-start | bytes 4616 | tf_op jit(solution)/shard_map/ppermute | solution.py:29
  423.6 63.8 %collective-permute-start.42 = (f32[2,1,128]{2,0,1:T(2,128)S(1)}, f32[2,1,128]{2,0,1:T(2,128)S(1)}, u32[]{:S(2)}, u32[]{:S(2)}) collective-permute-start(f32[2,1,128]{2,0,1:T(2,128)S(1)} %bitcast.1174), channel_id=1, source_target_pairs={{1,0},{2,1},{3,2},{4,3},{5,4},{6,5},{7,6},{8,7},{9,8},{10,9},{11,1... | collective-permute-start | bytes 3080 | tf_op jit(solution)/shard_map/ppermute | solution.py:29
  428.4 45.2 %collective-permute-start.50 = (f32[3,1,48]{2,0,1:T(4,128)S(1)}, f32[3,1,48]{2,0,1:T(4,128)S(1)}, u32[]{:S(2)}, u32[]{:S(2)}) collective-permute-start(f32[3,1,48]{2,0,1:T(4,128)S(1)} %add_bitcast_fusion.16), channel_id=1, source_target_pairs={{16,0},{32,16},{48,32},{64,48},{80,64},{96,80},{112,96},{128,112},... | collective-permute-start | bytes 1736 | tf_op jit(solution)/shard_map/ppermute | solution.py:29
  435.6 43.2 %collective-permute-start.51 = (f32[3,1,48]{2,0,1:T(4,128)S(1)}, f32[3,1,48]{2,0,1:T(4,128)S(1)}, u32[]{:S(2)}, u32[]{:S(2)}) collective-permute-start(f32[3,1,48]{2,0,1:T(4,128)S(1)} %add_bitcast_fusion.15), channel_id=1, source_target_pairs={{0,16},{16,32},{32,48},{48,64},{64,80},{80,96},{96,112},{112,128},... | collective-permute-start | bytes 1736 | tf_op jit(solution)/shard_map/ppermute | solution.py:27
  463.6 31.8 %collective-permute-start.48 = (f32[3,1,128]{2,0,1:T(4,128)S(1)}, f32[3,1,128]{2,0,1:T(4,128)S(1)}, u32[]{:S(2)}, u32[]{:S(2)}) collective-permute-start(f32[3,1,128]{2,0,1:T(4,128)S(1)} %add_bitcast_fusion.17), channel_id=1, source_target_pairs={{1,0},{2,1},{3,2},{4,3},{5,4},{6,5},{7,6},{8,7},{9,8},{10,9},{11,1... | collective-permute-start | bytes 4616 | tf_op jit(solution)/shard_map/ppermute | solution.py:29
  542.9 32.2 %collective-permute-start.56 = (f32[3,1,128]{2,0,1:T(4,128)S(1)}, f32[3,1,128]{2,0,1:T(4,128)S(1)}, u32[]{:S(2)}, u32[]{:S(2)}) collective-permute-start(f32[3,1,128]{2,0,1:T(4,128)S(1)} %add_bitcast_fusion.14), channel_id=1, source_target_pairs={{1,0},{2,1},{3,2},{4,3},{5,4},{6,5},{7,6},{8,7},{9,8},{10,9},{11,1... | collective-permute-start | bytes 4616 | tf_op jit(solution)/shard_map/ppermute | solution.py:29
  620.6 34.9 %collective-permute-start.64 = (f32[3,1,128]{2,0,1:T(4,128)S(1)}, f32[3,1,128]{2,0,1:T(4,128)S(1)}, u32[]{:S(2)}, u32[]{:S(2)}) collective-permute-start(f32[3,1,128]{2,0,1:T(4,128)S(1)} %add_bitcast_fusion.11), channel_id=1, source_target_pairs={{1,0},{2,1},{3,2},{4,3},{5,4},{6,5},{7,6},{8,7},{9,8},{10,9},{11,1... | collective-permute-start | bytes 4616 | tf_op jit(solution)/shard_map/ppermute | solution.py:29
  623.4 32.1 %collective-permute-start.65 = (f32[3,1,128]{2,0,1:T(4,128)S(1)}, f32[3,1,128]{2,0,1:T(4,128)S(1)}, u32[]{:S(2)}, u32[]{:S(2)}) collective-permute-start(f32[3,1,128]{2,0,1:T(4,128)S(1)} %get-tuple-element.433), channel_id=1, source_target_pairs={{0,1},{1,2},{2,3},{3,4},{4,5},{5,6},{6,7},{7,8},{8,9},{9,10},{10,1... | collective-permute-start | bytes 4616 | tf_op jit(solution)/shard_map/ppermute | solution.py:27
  660.9 34.8 %collective-permute-start.68 = (f32[2,1,128]{2,1,0:T(1,128)S(1)}, f32[2,1,128]{2,1,0:T(1,128)S(1)}, u32[]{:S(2)}, u32[]{:S(2)}) collective-permute-start(f32[2,1,128]{2,1,0:T(1,128)S(1)} %pad_add_fusion.60), channel_id=1, source_target_pairs={{1,0},{2,1},{3,2},{4,3},{5,4},{6,5},{7,6},{8,7},{9,8},{10,9},{11,1... | collective-permute-start | bytes 3080 | tf_op jit(solution)/shard_map/ppermute | solution.py:29
  740.8 34.8 %collective-permute-start.76 = (f32[2,1,128]{2,1,0:T(1,128)S(1)}, f32[2,1,128]{2,1,0:T(1,128)S(1)}, u32[]{:S(2)}, u32[]{:S(2)}) collective-permute-start(f32[2,1,128]{2,1,0:T(1,128)S(1)} %pad_add_fusion.58), channel_id=1, source_target_pairs={{1,0},{2,1},{3,2},{4,3},{5,4},{6,5},{7,6},{8,7},{9,8},{10,9},{11,1... | collective-permute-start | bytes 3080 | tf_op jit(solution)/shard_map/ppermute | solution.py:29
  781.1 36.7 %collective-permute-start.80 = (f32[3,1,128]{2,0,1:T(4,128)S(1)}, f32[3,1,128]{2,0,1:T(4,128)S(1)}, u32[]{:S(2)}, u32[]{:S(2)}) collective-permute-start(f32[3,1,128]{2,0,1:T(4,128)S(1)} %add_bitcast_fusion.5), channel_id=1, source_target_pairs={{1,0},{2,1},{3,2},{4,3},{5,4},{6,5},{7,6},{8,7},{9,8},{10,9},{11,1... | collective-permute-start | bytes 4616 | tf_op jit(solution)/shard_map/ppermute | solution.py:29
  867.0 34.8 %collective-permute-start.88 = (f32[3,1,128]{2,0,1:T(4,128)S(1)}, f32[3,1,128]{2,0,1:T(4,128)S(1)}, u32[]{:S(2)}, u32[]{:S(2)}) collective-permute-start(f32[3,1,128]{2,0,1:T(4,128)S(1)} %add_bitcast_fusion.2), channel_id=1, source_target_pairs={{1,0},{2,1},{3,2},{4,3},{5,4},{6,5},{7,6},{8,7},{9,8},{10,9},{11,1... | collective-permute-start | bytes 4616 | tf_op jit(solution)/shard_map/ppermute | solution.py:29
  868.9 32.9 %collective-permute-start.89 = (f32[3,1,128]{2,0,1:T(4,128)S(1)}, f32[3,1,128]{2,0,1:T(4,128)S(1)}, u32[]{:S(2)}, u32[]{:S(2)}) collective-permute-start(f32[3,1,128]{2,0,1:T(4,128)S(1)} %get-tuple-element.427), channel_id=1, source_target_pairs={{0,1},{1,2},{2,3},{3,4},{4,5},{5,6},{6,7},{7,8},{8,9},{9,10},{10,1... | collective-permute-start | bytes 4616 | tf_op jit(solution)/shard_map/ppermute | solution.py:27
  906.5 31.6 %collective-permute-start.95 = (f32[2,1,48]{2,0,1:T(2,128)S(1)}, f32[2,1,48]{2,0,1:T(2,128)S(1)}, u32[]{:S(2)}, u32[]{:S(2)}) collective-permute-start(f32[2,1,48]{2,0,1:T(2,128)S(1)} %bitcast.1178), channel_id=1, source_target_pairs={{0,16},{16,32},{32,48},{48,64},{64,80},{80,96},{96,112},{112,128},... | collective-permute-start | bytes 1160 | tf_op jit(solution)/shard_map/ppermute | solution.py:27
  909.2 43.9 %all-to-all-start.46 = ((f32[2,32,4]{2,0,1:T(2,128)}), f32[2,32,4]{2,0,1:T(2,128)S(1)}, u32[]{:S(2)}, u32[]{:S(2)}) async-start(f32[2,32,4]{2,0,1:T(2,128)} %copy.3961), calls=%async_computation.46 | async-start | bytes 65536 | tf_op jit(solution)/shard_map/all_to_all | solution.py:173
  916.5 64.2 %collective-permute-start.92 = (f32[2,1,128]{2,1,0:T(1,128)S(1)}, f32[2,1,128]{2,1,0:T(1,128)S(1)}, u32[]{:S(2)}, u32[]{:S(2)}) collective-permute-start(f32[2,1,128]{2,1,0:T(1,128)S(1)} %pad_add_fusion.54), channel_id=1, source_target_pairs={{1,0},{2,1},{3,2},{4,3},{5,4},{6,5},{7,6},{8,7},{9,8},{10,9},{11,1... | collective-permute-start | bytes 3080 | tf_op jit(solution)/shard_map/ppermute | solution.py:29
  919.6 61.1 %collective-permute-start.93 = (f32[2,1,128]{2,1,0:T(1,128)S(1)}, f32[2,1,128]{2,1,0:T(1,128)S(1)}, u32[]{:S(2)}, u32[]{:S(2)}) collective-permute-start(f32[2,1,128]{2,1,0:T(1,128)S(1)} %get-tuple-element.95), channel_id=1, source_target_pairs={{0,1},{1,2},{2,3},{3,4},{4,5},{5,6},{6,7},{7,8},{8,9},{9,10},{10,1... | collective-permute-start | bytes 3080 | tf_op jit(solution)/shard_map/ppermute | solution.py:27
  934.1 54.7 %collective-permute-start.46 = (f32[3,1,128]{2,1,0:T(1,128)S(1)}, f32[3,1,128]{2,1,0:T(1,128)S(1)}, u32[]{:S(2)}, u32[]{:S(2)}) collective-permute-start(f32[3,1,128]{2,1,0:T(1,128)S(1)} %get-tuple-element.287), channel_id=1, source_target_pairs={{1,0},{2,1},{3,2},{4,3},{5,4},{6,5},{7,6},{8,7},{9,8},{10,9},{11,1... | collective-permute-start | bytes 4616 | tf_op jit(solution)/shard_map/ppermute | solution.py:29
  (126 other events, 2225.4 us)
where the time goes:
time: 1000 us; the launch traced here: 990 us
  starting transfers between devices  709 us (71%)
  waiting for transfers between devices  209 us (21%)
  local copies, waits for them, and re-layouts  50.3 us (5%)
  other arithmetic  15.5 us (2%)
    ppermute x48, starting transfers between devices, extended_2(): lax.ppermute(head, axis, [((i + 1) % count, i) for i in range(ends)])  274 us
    ppermute x48, starting transfers between devices, extended_2(): lax.ppermute(tail, axis, [(i, (i + 1) % count) for i in range(ends)])  171 us
    all_to_all x24, starting transfers between devices, reverse_sources(): lax.all_to_all(jnp.flip(received, 1), 'lon', split_axis=1, concat_axis=1,...  148 us
    all_to_all x24, waiting for transfers between devices, reverse_sources(): lax.all_to_all(jnp.flip(received, 1), 'lon', split_axis=1, concat_axis=1,...  143 us
    all_to_all x24, starting transfers between devices, mirror(): lax.all_to_all(pieces, 'lon', split_axis=1, concat_axis=1, tiled=True)  116 us
    ppermute x48, waiting for transfers between devices, extended_2(): lax.ppermute(tail, axis, [(i, (i + 1) % count) for i in range(ends)])  50.4 us
  transfers between devices with their start and end apart: 144, of which 38 were waited for; matrix products, arithmetic and copies ran while one was open for 4% of the time, Pallas kernels for 0%

commit v1 on v0

v1 whole, which is shorter than its diff:
```python
from functools import partial

import jax
import jax.numpy as jnp
from jax import lax
from jax.experimental import pallas as pl
from jax.experimental.pallas import tpu as pltpu
from jax.sharding import PartitionSpec as P

NSUB = 6
EVP_TOTAL = 120
MESH = pl.DeviceIdType.MESH

ROWS = 48
COLS = 128
PAD = 24
EXT = ROWS + 2 * PAD
REACH = 22
BACK = 12
NFLD = 11
NMAIN = 9
SLOT = 24

ODD_FIELDS = (0, 1, 7, 8, 9, 10)


def slot_of(field):
    if field < 5:
        return 0, SLOT * field, SLOT
    if field < NMAIN:
        return 1, SLOT * (field - 5), SLOT
    return 1, 4 * SLOT + BACK * (field - NMAIN), BACK


def lane_ids(shape):
    return lax.broadcasted_iota(jnp.int32, shape, len(shape) - 1)


def gather_kernel(
    lon_count,
    lat_count,
    vel,
    sig,
    strength,
    wind,
    mask,
    cot,
    ext,
    land,
    sig_in,
    str_in,
    wind_in,
    mask_in,
    pack,
    local_sem,
    send_sem,
    recv_sem,
    self_sem,
):
    lon = lax.axis_index("lon")
    lat = lax.axis_index("lat")
    top = lat == lat_count - 1
    bottom = lat == 0
    west = lax.rem(lon + lon_count - 1, lon_count)
    east = lax.rem(lon + 1, lon_count)
    up = jnp.where(top, lat, lat + 1)
    down = jnp.where(bottom, lat, lat - 1)
    north_lon = jnp.where(top, lon_count - 1 - lon, lon)
    north_a = jnp.where(top, lax.rem(lon_count - lon, lon_count), west)
    north_b = jnp.where(top, lax.rem(2 * lon_count - 2 - lon, lon_count), east)
    self_a = jnp.logical_and(top, north_a == lon)
    self_b = jnp.logical_and(top, north_b == lon)

    barrier = pltpu.get_barrier_semaphore()

    def greet(dev_lon, dev_lat):
        pl.semaphore_signal(barrier, inc=1, device_id=(dev_lon, dev_lat), device_id_type=MESH)

    greet(west, lat)
    greet(east, lat)
    greet(north_lon, up)
    pl.when(jnp.logical_not(self_a))(lambda: greet(north_a, up))
    pl.when(jnp.logical_not(self_b))(lambda: greet(north_b, up))

    @pl.when(jnp.logical_not(bottom))
    def _():
        greet(lon, down)
        greet(west, down)
        greet(east, down)

    own = pl.ds(PAD, ROWS)
    loads = [
        pltpu.make_async_copy(vel, ext.at[pl.ds(0, 2), own], local_sem.at[0]),
        pltpu.make_async_copy(sig, sig_in, local_sem.at[1]),
        pltpu.make_async_copy(strength, str_in, local_sem.at[2]),
        pltpu.make_async_copy(wind, wind_in, local_sem.at[3]),
        pltpu.make_async_copy(mask, mask_in, local_sem.at[4]),
        pltpu.make_async_copy(cot, ext.at[pl.ds(NMAIN, 2), own], local_sem.at[5]),
    ]
    for copy in loads:
        copy.start()
    for copy in loads:
        copy.wait()

    cover = mask_in[...].astype(jnp.float32)
    ext[2, own] = 0.125 * (sig_in[0] + sig_in[1])
    ext[3, own] = 0.125 * (sig_in[0] - sig_in[1])
    ext[4, own] = 0.25 * sig_in[2]
    ext[5, own] = (1.0 / 24.0) * cover * str_in[...]
    ext[6, own] = cover * (1.0 / 1.5)
    ext[7, own] = wind_in[0].astype(jnp.float32)
    ext[8, own] = wind_in[1].astype(jnp.float32)

    lanes = lane_ids((ROWS, COLS))
    for side in range(2):
        for plane in range(2):
            packed = None
            for field in range(NFLD):
                at_plane, first, width = slot_of(field)
                if at_plane != plane:
                    continue
                begin = 0 if side == 0 else COLS - width
                value = ext[field, own]
                shift = (first - begin) % COLS
                if shift:
                    value = pltpu.roll(value, shift, 1)
                packed = value if packed is None else jnp.where(lanes < first, packed, value)
            pack[side, plane] = packed

    @pl.when(bottom)
    def _():
        ext[:, pl.ds(0, PAD)] = jnp.zeros((NFLD, PAD, COLS), jnp.float32)
        land[:, :, pl.ds(0, PAD)] = jnp.zeros((2, 2, PAD, COLS), jnp.float32)

    count = (
        3
        + jnp.where(self_a, 0, 1)
        + jnp.where(self_b, 0, 1)
        + jnp.where(bottom, 0, 3)
    )
    pl.semaphore_wait(barrier, count)

    def send(src, dst, slot, sem, dev_lon, dev_lat):
        return pltpu.make_async_remote_copy(
            src_ref=src,
            dst_ref=dst,
            send_sem=send_sem.at[slot],
            recv_sem=recv_sem.at[sem],
            device_id=(dev_lon, dev_lat),
            device_id_type=MESH,
        )

    main = pl.ds(0, NMAIN)
    tail = pl.ds(NMAIN, 2)
    def north_sends(row_main, row_tail, sem):
        return (
            send(ext.at[main, pl.ds(PAD + ROWS - REACH, REACH)], ext.at[main, pl.ds(row_main, REACH)], 0, sem, north_lon, up),
            send(ext.at[tail, pl.ds(PAD + ROWS - BACK, BACK)], ext.at[tail, pl.ds(row_tail, BACK)], 1, sem + 1, north_lon, up),
        )

    def north_strip(side, row, sem, dev_lon):
        return send(
            pack.at[side, :, pl.ds(ROWS - REACH, REACH)], land.at[side, :, pl.ds(row, REACH)], 2 + side, sem, dev_lon, up
        )

    def north_self(side):
        return pltpu.make_async_copy(
            pack.at[side, :, pl.ds(ROWS - REACH, REACH)],
            land.at[side, :, pl.ds(EXT - REACH, REACH)],
            self_sem.at[side],
        )

    south_sends = (
        send(ext.at[main, pl.ds(PAD, REACH)], ext.at[main, pl.ds(PAD + ROWS, REACH)], 4, 2, lon, down),
        send(ext.at[tail, pl.ds(PAD, BACK)], ext.at[tail, pl.ds(PAD + ROWS, BACK)], 5, 3, lon, down),
        send(pack.at[0, :, pl.ds(0, REACH)], land.at[0, :, pl.ds(PAD + ROWS, REACH)], 6, 4, west, down),
        send(pack.at[1, :, pl.ds(0, REACH)], land.at[1, :, pl.ds(PAD + ROWS, REACH)], 7, 5, east, down),
    )
    lon_sends = (
        send(pack.at[0], land.at[0, :, own], 8, 0, west, lat),
        send(pack.at[1], land.at[1, :, own], 9, 1, east, lat),
    )
    low = north_sends(PAD - REACH, PAD - BACK, 6)
    fold = north_sends(EXT - REACH, EXT - BACK, 2)
    low_strips = (north_strip(0, PAD - REACH, 8, north_a), north_strip(1, PAD - REACH, 9, north_b))
    fold_strips = (north_strip(0, EXT - REACH, 4, north_a), north_strip(1, EXT - REACH, 5, north_b))

    @pl.when(jnp.logical_not(top))
    def _():
        for copy in low + low_strips:
            copy.start()

    @pl.when(top)
    def _():
        for copy in fold:
            copy.start()
        for side, is_self in ((0, self_a), (1, self_b)):
            pl.when(is_self)(lambda side=side: north_self(side).start())
            pl.when(jnp.logical_not(is_self))(lambda side=side: fold_strips[side].start())

    @pl.when(jnp.logical_not(bottom))
    def _():
        for copy in south_sends:
            copy.start()

    for copy in lon_sends:
        copy.start()

    lon_sends[0].wait_recv()
    lon_sends[1].wait_recv()
    south_sends[0].wait_recv()
    south_sends[1].wait_recv()
    for side, is_self in ((0, self_a), (1, self_b)):
        pl.when(is_self)(lambda side=side: north_self(side).wait())
        pl.when(jnp.logical_not(is_self))(lambda side=side: south_sends[2 + side].wait_recv())

    @pl.when(jnp.logical_not(bottom))
    def _():
        for copy in low + low_strips:
            copy.wait_recv()
        for copy in south_sends:
            copy.wait_send()

    for copy in low:
        copy.wait_send()
    for side, is_self in ((0, self_a), (1, self_b)):
        pl.when(jnp.logical_not(is_self))(lambda side=side: low_strips[side].wait_send())
    for copy in lon_sends:
        copy.wait_send()


def gather_halos(lon_count, lat_count, *operands):
    f32 = jnp.float32
    return pl.pallas_call(
        partial(gather_kernel, lon_count, lat_count),
        out_shape=(
            jax.ShapeDtypeStruct((NFLD, EXT, COLS), f32),
            jax.ShapeDtypeStruct((2, 2, EXT, COLS), f32),
        ),
        in_specs=[pl.BlockSpec(memory_space=pl.ANY)] * 6,
        out_specs=(
            pl.BlockSpec(memory_space=pltpu.VMEM),
            pl.BlockSpec(memory_space=pltpu.VMEM),
        ),
        scratch_shapes=[
            pltpu.VMEM((3, ROWS, COLS), f32),
            pltpu.VMEM((ROWS, COLS), f32),
            pltpu.VMEM((2, ROWS, COLS), jnp.bfloat16),
            pltpu.VMEM((ROWS, COLS), jnp.int32),
            pltpu.VMEM((2, 2, ROWS, COLS), f32),
            pltpu.SemaphoreType.DMA((6,)),
            pltpu.SemaphoreType.DMA((10,)),
            pltpu.SemaphoreType.DMA((10,)),
            pltpu.SemaphoreType.DMA((2,)),
        ],
        compiler_params=pltpu.CompilerParams(
            collective_id=0, has_side_effects=True, vmem_limit_bytes=32 * 1024 * 1024
        ),
    )(*operands)


TILE = 8


def tiles_for(reach):
    low = (PAD - reach) // TILE
    high = -(-(PAD + ROWS + reach) // TILE)
    return range(low * TILE, high * TILE, TILE)


def flip_tile(value):
    lane = lane_ids(value.shape)
    bit = 1
    while bit < COLS:
        value = jnp.where((lane & bit) != 0, pltpu.roll(value, bit, 1), pltpu.roll(value, COLS - bit, 1))
        bit *= 2
    row = lax.broadcasted_iota(jnp.int32, value.shape, 0)
    bit = 1
    while bit < TILE:
        value = jnp.where((row & bit) != 0, pltpu.roll(value, bit, 0), pltpu.roll(value, TILE - bit, 0))
        bit *= 2
    return value


def evp_kernel(
    lat_count,
    start,
    ext,
    land,
    final_vel,
    vel_grad,
    sig_grad,
    fld,
    state,
    turn,
    saved,
    back,
    strain,
    carry,
):
    top = lax.axis_index("lat") == lat_count - 1
    band = lax.axis_index("lat")
    shape = (TILE, COLS)
    lane = lane_ids(shape)
    first_lane = lane == 0
    last_lane = lane == COLS - 1
    west_half = lane < COLS // 2

    for r in range(0, EXT, TILE):
        rows = pl.ds(r, TILE)
        for field in range(NFLD):
            plane, first, width = slot_of(field)
            a = land[0, plane, rows]
            b = land[1, plane, rows]
            shift_a = (-first) % COLS
            shift_b = (COLS - width - first) % COLS
            if shift_a:
                a = pltpu.roll(a, shift_a, 1)
            if shift_b:
                b = pltpu.roll(b, shift_b, 1)
            fld[field, 0, rows] = ext[field, rows]
            fld[field, 1, rows] = jnp.where(west_half, a, b)

    @pl.when(top)
    def _():
        def one(i, _):
            odd = (i < 2) | (i >= 7)
            sign = jnp.where(odd, -1.0, 1.0)
            for plane in range(2):
                old = [fld[i, plane, pl.ds(PAD + ROWS + t * TILE, TILE)] for t in range(3)]
                for t in range(3):
                    fld[i, plane, pl.ds(PAD + ROWS + t * TILE, TILE)] = sign * flip_tile(old[2 - t])
            return 0

        lax.fori_loop(0, NFLD, one, 0)

    for r in range(0, EXT, TILE):
        rows = pl.ds(r, TILE)
        row = band * ROWS + (r - PAD) + lax.broadcasted_iota(jnp.int32, shape, 0)
        total = ROWS * lat_count
        row = jnp.where(row >= total, 2 * total - 1 - row, row).astype(jnp.float32)
        half_f = 0.6 * ((2.0 * row + 1.0) / total - 1.0)
        scale = 1.5 / (2.25 + half_f * half_f)
        for plane in range(2):
            cover = fld[6, plane, rows]
            turn[0, plane, rows] = cover * (1.5 * scale)
            turn[1, plane, rows] = cover * (half_f * scale)

    def at(ref, lead, plane, r):
        if r < 0:
            return pltpu.roll(ref[lead + (plane, pl.ds(0, TILE))], 1, 0)
        if r > EXT - TILE:
            return pltpu.roll(ref[lead + (plane, pl.ds(EXT - TILE, TILE))], TILE - 1, 0)
        return ref[lead + (plane, pl.ds(r, TILE))]

    def lat_diff(ref, lead, r):
        return [at(ref, lead, p, r + 1) - at(ref, lead, p, r - 1) for p in range(2)]

    def lon_diff(ref, lead, r):
        here = [at(ref, lead, p, r) for p in range(2)]
        east = [pltpu.roll(x, COLS - 1, 1) for x in here]
        west = [pltpu.roll(x, 1, 1) for x in here]
        return [
            jnp.where(last_lane, east[1 - p], east[p]) - jnp.where(first_lane, west[1 - p], west[p])
            for p in range(2)
        ]

    start_value = start[0].astype(jnp.float32)
    for k in range(NSUB):
        src = fld if k == 0 else state
        left = NSUB - 1 - k
        keep = set(tiles_for(2 * k + 1))
        for r in tiles_for(11 + 2 * left):
            rows = pl.ds(r, TILE)
            dux = lon_diff(src, (0,), r)
            dvx = lon_diff(src, (1,), r)
            duy = lat_diff(src, (0,), r)
            dvy = lat_diff(src, (1,), r)
            for p in range(2):
                div = dux[p] + dvy[p]
                ten = dux[p] - dvy[p]
                she = duy[p] + dvx[p]
                inv = lax.rsqrt(div * div + 0.25 * (ten * ten + she * she) + 1.0)
                part = fld[5, p, rows]
                div = div * inv
                inv4 = 0.25 * inv
                ten = ten * inv4
                she = she * inv4
                if r in keep:
                    saved[k, 0, p, rows] = div
                    saved[k, 1, p, rows] = ten
                    saved[k, 2, p, rows] = she
                    saved[k, 3, p, rows] = part * inv
                cover = fld[6, p, rows]
                pull = div - 1.0
                state[2, p, rows] = cover * src[2, p, rows] + part * (pull + ten)
                state[3, p, rows] = cover * src[3, p, rows] + part * (pull - ten)
                state[4, p, rows] = cover * src[4, p, rows] + part * she
        weight = 0.5 * ((start_value + (k + 1)) / EVP_TOTAL)
        for r in tiles_for(0 if left == 0 else 10 + 2 * left):
            rows = pl.ds(r, TILE)
            dxx = lon_diff(state, (2,), r)
            dxy = lon_diff(state, (4,), r)
            dyx = lat_diff(state, (4,), r)
            dyy = lat_diff(state, (3,), r)
            for p in range(2):
                ru = src[0, p, rows] + (dxx[p] + dyx[p]) + weight * fld[7, p, rows]
                rv = src[1, p, rows] + (dxy[p] + dyy[p]) + weight * fld[8, p, rows]
                ca = turn[0, p, rows]
                cb = turn[1, p, rows]
                un = ca * ru + cb * rv
                vn = ca * rv - cb * ru
                if left == 0:
                    if p == 0:
                        final_vel[0, pl.ds(r - PAD, TILE)] = un
                        final_vel[1, pl.ds(r - PAD, TILE)] = vn
                else:
                    state[0, p, rows] = un
                    state[1, p, rows] = vn

    for r in tiles_for(BACK):
        rows = pl.ds(r, TILE)
        for p in range(2):
            gu = fld[9, p, rows]
            gv = fld[10, p, rows]
            ca = turn[0, p, rows]
            cb = turn[1, p, rows]
            back[0, p, rows] = ca * gu - cb * gv
            back[1, p, rows] = cb * gu + ca * gv

    for k in reversed(range(NSUB)):
        for r in tiles_for(2 * k + 1):
            rows = pl.ds(r, TILE)
            dux = lon_diff(back, (0,), r)
            dvx = lon_diff(back, (1,), r)
            duy = lat_diff(back, (0,), r)
            dvy = lat_diff(back, (1,), r)
            for p in range(2):
                gx = -dux[p]
                gy = -dvy[p]
                gz = -(duy[p] + dvx[p])
                if k < NSUB - 1:
                    gx = carry[0, p, rows] + gx
                    gy = carry[1, p, rows] + gy
                    gz = carry[2, p, rows] + gz
                both = gx + gy
                apart = gx - gy
                cover = fld[6, p, rows]
                if k > 0:
                    carry[0, p, rows] = cover * gx
                    carry[1, p, rows] = cover * gy
                    carry[2, p, rows] = cover * gz
                elif p == 0 and PAD <= r < PAD + ROWS:
                    out = pl.ds(r - PAD, TILE)
                    c8 = 0.125 * cover
                    sig_grad[0, out] = c8 * both
                    sig_grad[1, out] = c8 * apart
                    sig_grad[2, out] = (0.25 * cover) * gz
                div = saved[k, 0, p, rows]
                ten = saved[k, 1, p, rows]
                she = saved[k, 2, p, rows]
                part = saved[k, 3, p, rows]
                along = both * div + apart * ten + gz * she
                g_div = part * (both - along * div)
                g_ten = part * (0.25 * apart - along * ten)
                strain[0, p, rows] = g_div + g_ten
                strain[1, p, rows] = g_div - g_ten
                strain[2, p, rows] = part * (0.25 * gz - along * she)
        for r in tiles_for(2 * k):
            rows = pl.ds(r, TILE)
            dax = lon_diff(strain, (0,), r)
            dsx = lon_diff(strain, (2,), r)
            dsy = lat_diff(strain, (2,), r)
            dby = lat_diff(strain, (1,), r)
            for p in range(2):
                gu = back[0, p, rows] - (dax[p] + dsy[p])
                gv = back[1, p, rows] - (dsx[p] + dby[p])
                if k > 0:
                    ca = turn[0, p, rows]
                    cb = turn[1, p, rows]
                    back[0, p, rows] = ca * gu - cb * gv
                    back[1, p, rows] = cb * gu + ca * gv
                elif p == 0:
                    vel_grad[0, pl.ds(r - PAD, TILE)] = gu
                    vel_grad[1, pl.ds(r - PAD, TILE)] = gv


def evp_and_adjoint(lat_count, start, ext, land):
    f32 = jnp.float32
    vmem = pl.BlockSpec(memory_space=pltpu.VMEM)
    return pl.pallas_call(
        partial(evp_kernel, lat_count),
        out_shape=(
            jax.ShapeDtypeStruct((2, ROWS, COLS), f32),
            jax.ShapeDtypeStruct((2, ROWS, COLS), f32),
            jax.ShapeDtypeStruct((3, ROWS, COLS), f32),
        ),
        in_specs=[pl.BlockSpec(memory_space=pltpu.SMEM), vmem, vmem],
        out_specs=(vmem, vmem, vmem),
        scratch_shapes=[
            pltpu.VMEM((NFLD, 2, EXT, COLS), f32),
            pltpu.VMEM((5, 2, EXT, COLS), f32),
            pltpu.VMEM((2, 2, EXT, COLS), f32),
            pltpu.VMEM((NSUB, 4, 2, EXT, COLS), f32),
            pltpu.VMEM((2, 2, EXT, COLS), f32),
            pltpu.VMEM((3, 2, EXT, COLS), f32),
            pltpu.VMEM((3, 2, EXT, COLS), f32),
        ],
        compiler_params=pltpu.CompilerParams(vmem_limit_bytes=32 * 1024 * 1024),
    )(start, ext, land)


def shards(lon_count, lat_count, velocity, stress, strength, wind_stress, ice_mask, start_step, velocity_cotangent):
    ext, land = gather_halos(
        lon_count, lat_count, velocity, stress, strength, wind_stress, ice_mask, velocity_cotangent
    )
    return evp_and_adjoint(lat_count, start_step, ext, land)


def solution(mesh):
    placed = (
        P(None, "lat", "lon"),
        P(None, "lat", "lon"),
        P("lat", "lon"),
        P(None, "lat", "lon"),
        P("lat", "lon"),
        P(),
        P(None, "lat", "lon"),
    )
    return jax.shard_map(
        partial(shards, mesh.shape["lon"], mesh.shape["lat"]),
        mesh=mesh,
        in_specs=placed,
        out_specs=(P(None, "lat", "lon"), P(None, "lat", "lon"), P(None, "lat", "lon")),
        check_vma=False,
    )
```

time: 1000 us -> 43.6 us (0.04)
  the two profiles are of different devices: /device:TPU:6 before, /device:TPU:390 now
where the time goes in v1:
time: 43.6 us; the launch traced here: 43.1 us
  Pallas kernels  37.1 us (85%)
  local copies, waits for them, and re-layouts  4.68 us (11%)
  between operations  1.3 us (3%)
    pallas_call x1, Pallas kernels, gather_halos(): pl.pallas_call(partial(gather_kernel, lon_count, lat_count), out_shape=(j...  28.4 us
    pallas_call x1, Pallas kernels, evp_and_adjoint(): pl.pallas_call(partial(evp_kernel, lat_count), out_shape=(jax.ShapeDtypeS...  8.75 us
    unnamed x12, local copies, waits for them, and re-layouts  4.68 us

profile of v1, /device:TPU:390, one launch (start us, length us, event | category | flops | bytes accessed | tf_op | source)
XLA Modules:
  0.0 43.1 jit_solution(391763698057041205)
XLA Ops:
  1.3 0.0 copy-start
  1.3 0.9 %copy-done = f32[3,48,128]{2,1,0:T(8,128)S(1)} copy-done((f32[3,48,128]{2,1,0:T(8,128)S(1)}, f32[3,48,128]{2,1,0:T(8,128)}, u32[]{:S(2)}) %copy-start) | copy-done | bytes 73752
  2.2 0.0 copy-start.1
  2.2 0.8 %copy-done.1 = f32[2,48,128]{2,1,0:T(8,128)S(1)} copy-done((f32[2,48,128]{2,1,0:T(8,128)S(1)}, f32[2,48,128]{2,1,0:T(8,128)}, u32[]{:S(2)}) %copy-start.1) | copy-done | bytes 49176
  3.0 0.0 copy-start.2
  3.0 0.8 %copy-done.2 = f32[2,48,128]{2,1,0:T(8,128)S(1)} copy-done((f32[2,48,128]{2,1,0:T(8,128)S(1)}, f32[2,48,128]{2,1,0:T(8,128)}, u32[]{:S(2)}) %copy-start.2) | copy-done | bytes 49176
  3.8 0.0 copy-start.3
  3.8 0.7 %copy-done.3 = f32[48,128]{1,0:T(8,128)S(1)} copy-done((f32[48,128]{1,0:T(8,128)S(1)}, f32[48,128]{1,0:T(8,128)}, u32[]{:S(2)}) %copy-start.3) | copy-done | bytes 24600
  4.5 0.0 copy-start.4
  4.5 0.7 %copy-done.4 = bf16[2,48,128]{2,1,0:T(8,128)(2,1)S(1)} copy-done((bf16[2,48,128]{2,1,0:T(8,128)(2,1)S(1)}, bf16[2,48,128]{2,1,0:T(8,128)(2,1)}, u32[]{:S(2)}) %copy-start.4) | copy-done | bytes 24600
  5.2 0.0 copy-start.5
  5.2 0.7 %copy-done.5 = s32[48,128]{1,0:T(8,128)S(1)} copy-done((s32[48,128]{1,0:T(8,128)S(1)}, s32[48,128]{1,0:T(8,128)}, u32[]{:S(2)}) %copy-start.5) | copy-done | bytes 24600
  6.0 28.4 %shard_map.94 = (f32[11,96,128]{2,1,0:T(8,128)S(1)}, f32[2,2,96,128]{3,2,1,0:T(8,128)S(1)}) custom-call(f32[2,48,128]{2,1,0:T(8,128)S(1)} %copy-done.1, f32[3,48,128]{2,1,0:T(8,128)S(1)} %copy-done, f32[48,128]{1,0:T(8,128)S(1)} %copy-done.3, bf16[2,48,128]{2,1,0:T(8,128)(2,1)S(1)} %copy-done.4, s32[48,128]{1,0:T(8,128)S(1)} %copy-done.5, ...), custom_call_target="tpu_custom_call" | custom-call | tf_op jit(solution)/shard_map/pallas_call | solution.py:234
  34.4 8.7 %shard_map.95 = (f32[2,48,128]{2,1,0:T(8,128)}, f32[2,48,128]{2,1,0:T(8,128)}, f32[3,48,128]{2,1,0:T(8,128)}) custom-call(s32[1]{0:T(128)S(6)} %copy.10.start, f32[11,96,128]{2,1,0:T(8,128)S(1)} %get-tuple-element.5.ext, f32[2,2,96,128]{3,2,1,0:T(8,128)S(1)} %get-tuple-element.6.land), custom_call_target="tpu_custom_call" | custom-call | tf_op jit(solution)/shard_map/pallas_call | solution.py:491
Async XLA Ops:
  1.3 0.9 %copy-start = (f32[3,48,128]{2,1,0:T(8,128)S(1)}, f32[3,48,128]{2,1,0:T(8,128)}, u32[]{:S(2)}) copy-start(f32[3,48,128]{2,1,0:T(8,128)} %sig.1) | copy-start | bytes 221188
  2.2 0.8 %copy-start.1 = (f32[2,48,128]{2,1,0:T(8,128)S(1)}, f32[2,48,128]{2,1,0:T(8,128)}, u32[]{:S(2)}) copy-start(f32[2,48,128]{2,1,0:T(8,128)} %vel.1) | copy-start | bytes 147460
  3.0 0.8 %copy-start.2 = (f32[2,48,128]{2,1,0:T(8,128)S(1)}, f32[2,48,128]{2,1,0:T(8,128)}, u32[]{:S(2)}) copy-start(f32[2,48,128]{2,1,0:T(8,128)} %cot.1) | copy-start | bytes 147460
  3.8 0.7 %copy-start.3 = (f32[48,128]{1,0:T(8,128)S(1)}, f32[48,128]{1,0:T(8,128)}, u32[]{:S(2)}) copy-start(f32[48,128]{1,0:T(8,128)} %strength.1) | copy-start | bytes 73732
  4.5 0.7 %copy-start.4 = (bf16[2,48,128]{2,1,0:T(8,128)(2,1)S(1)}, bf16[2,48,128]{2,1,0:T(8,128)(2,1)}, u32[]{:S(2)}) copy-start(bf16[2,48,128]{2,1,0:T(8,128)(2,1)} %wind.1) | copy-start | bytes 73732
  5.2 0.7 %copy-start.5 = (s32[48,128]{1,0:T(8,128)S(1)}, s32[48,128]{1,0:T(8,128)}, u32[]{:S(2)}) copy-start(s32[48,128]{1,0:T(8,128)} %mask.1) | copy-start | bytes 73732

commit v2 on v1

--- a/solution.py
+++ b/solution.py
@@ -10,6 +10,7 @@
 NSUB = 6
 EVP_TOTAL = 120
 MESH = pl.DeviceIdType.MESH
+VMEM_LIMIT = 60 * 1024 * 1024
 
 ROWS = 48
 COLS = 128
@@ -34,6 +35,17 @@
 
 def lane_ids(shape):
     return lax.broadcasted_iota(jnp.int32, shape, len(shape) - 1)
+
+
+def start_order(lon, lat):
+    y = lax.div(lon, 8)
+    z_low = lax.rem(lax.div(lon, 2), 4)
+    x = lax.div(lat, 4)
+    z_high = lax.rem(lat, 4)
+    early_half = z_high < 2
+    base = jnp.where(early_half, 44 * z_high, 96 - 4 * z_high)
+    step = jnp.where(early_half, 13, 4)
+    return 1024 * (7 * x + 7 * y + base + step * z_low) + 32 * lat + lon
 
 
 def gather_kernel(
@@ -47,214 +59,275 @@
     cot,
     ext,
     land,
+    wind_in,
+    mask_in,
+    vel_in,
     sig_in,
     str_in,
-    wind_in,
-    mask_in,
+    cot_in,
+    made,
     pack,
     local_sem,
     send_sem,
     recv_sem,
     self_sem,
+    ready,
 ):
     lon = lax.axis_index("lon")
     lat = lax.axis_index("lat")
     top = lat == lat_count - 1
-    bottom = lat == 0
+    inner = jnp.logical_not(top)
+    has_south = lat > 0
     west = lax.rem(lon + lon_count - 1, lon_count)
     east = lax.rem(lon + 1, lon_count)
     up = jnp.where(top, lat, lat + 1)
-    down = jnp.where(bottom, lat, lat - 1)
+    down = jnp.where(has_south, lat - 1, lat)
     north_lon = jnp.where(top, lon_count - 1 - lon, lon)
     north_a = jnp.where(top, lax.rem(lon_count - lon, lon_count), west)
     north_b = jnp.where(top, lax.rem(2 * lon_count - 2 - lon, lon_count), east)
     self_a = jnp.logical_and(top, north_a == lon)
     self_b = jnp.logical_and(top, north_b == lon)
+    always = lat >= 0
+
+    W, E, N, NA, NB, S, SA, SB = range(8)
+    partner = [
+        (west, lat),
+        (east, lat),
+        (north_lon, up),
+        (north_a, up),
+        (north_b, up),
+        (lon, down),
+        (west, down),
+        (east, down),
+    ]
+    there = [always, always, always, jnp.logical_not(self_a), jnp.logical_not(self_b), has_south, has_south, has_south]
+    reverse = [
+        E,
+        W,
+        jnp.where(top, N, S),
+        jnp.where(top, NA, SB),
+        jnp.where(top, NB, SA),
+        N,
+        NB,
+        NA,
+    ]
+    mine = start_order(lon, lat)
+    later = [start_order(*p) > mine for p in partner]
+    greets = [jnp.logical_and(t, l) for t, l in zip(there, later)]
+    greeted = [jnp.logical_and(t, jnp.logical_not(l)) for t, l in zip(there, later)]
 
     barrier = pltpu.get_barrier_semaphore()
-
-    def greet(dev_lon, dev_lat):
-        pl.semaphore_signal(barrier, inc=1, device_id=(dev_lon, dev_lat), device_id_type=MESH)
-
-    greet(west, lat)
-    greet(east, lat)
-    greet(north_lon, up)
-    pl.when(jnp.logical_not(self_a))(lambda: greet(north_a, up))
-    pl.when(jnp.logical_not(self_b))(lambda: greet(north_b, up))
-
-    @pl.when(jnp.logical_not(bottom))
-    def _():
-        greet(lon, down)
-        greet(west, down)
-        greet(east, down)
+    for link in range(8):
+
+        @pl.when(greets[link])
+        def _(link=link):
+            pl.semaphore_signal(barrier, inc=1, device_id=partner[link], device_id_type=MESH)
 
     own = pl.ds(PAD, ROWS)
     loads = [
-        pltpu.make_async_copy(vel, ext.at[pl.ds(0, 2), own], local_sem.at[0]),
-        pltpu.make_async_copy(sig, sig_in, local_sem.at[1]),
-        pltpu.make_async_copy(strength, str_in, local_sem.at[2]),
-        pltpu.make_async_copy(wind, wind_in, local_sem.at[3]),
-        pltpu.make_async_copy(mask, mask_in, local_sem.at[4]),
-        pltpu.make_async_copy(cot, ext.at[pl.ds(NMAIN, 2), own], local_sem.at[5]),
+        pltpu.make_async_copy(wind, wind_in, local_sem.at[0]),
+        pltpu.make_async_copy(mask, mask_in, local_sem.at[1]),
+        pltpu.make_async_copy(vel, vel_in, local_sem.at[2]),
+        pltpu.make_async_copy(sig, sig_in, local_sem.at[3]),
+        pltpu.make_async_copy(strength, str_in, local_sem.at[4]),
+        pltpu.make_async_copy(cot, cot_in, local_sem.at[5]),
     ]
     for copy in loads:
         copy.start()
+
+    def send(src, dst, slot, sem, link):
+        return pltpu.make_async_remote_copy(
+            src_ref=src,
+            dst_ref=dst,
+            send_sem=send_sem.at[slot],
+            recv_sem=recv_sem.at[sem],
+            device_id=partner[link],
+            device_id_type=MESH,
+        )
+
+    def rows_raw(row_of, to_of, slot, sem, link):
+        return [
+            send(vel.at[:, pl.ds(row_of(REACH), REACH)], ext.at[pl.ds(0, 2), pl.ds(to_of(REACH), REACH)], slot, sem, link),
+            send(
+                sig.at[:, pl.ds(row_of(REACH - 1), REACH - 1)],
+                ext.at[pl.ds(2, 3), pl.ds(to_of(REACH - 1), REACH - 1)],
+                slot + 1,
+                sem + 1,
+                link,
+            ),
+            send(
+                strength.at[pl.ds(row_of(REACH - 1), REACH - 1)],
+                ext.at[5, pl.ds(to_of(REACH - 1), REACH - 1)],
+                slot + 2,
+                sem + 2,
+                link,
+            ),
+            send(cot.at[:, pl.ds(row_of(BACK), BACK)], ext.at[pl.ds(NMAIN, 2), pl.ds(to_of(BACK), BACK)], slot + 3, sem + 3, link),
+        ]
+
+    def rows_made(row_of, to_of, slot, sem, link):
+        return send(
+            made.at[:, pl.ds(row_of(REACH - 1), REACH - 1)],
+            ext.at[pl.ds(6, 3), pl.ds(to_of(REACH - 1), REACH - 1)],
+            slot + 4,
+            sem + 4,
+            link,
+        )
+
+    last = lambda n: ROWS - n
+    to_low = lambda n: PAD - n
+    to_fold = lambda n: EXT - n
+    first = lambda n: 0
+    to_high = lambda n: PAD + ROWS
+
+    def strip(side, row, to, slot, sem, link):
+        return send(pack.at[side, :, pl.ds(row, REACH)], land.at[side, :, pl.ds(to, REACH)], slot, sem, link)
+
+    def self_strip(side):
+        return pltpu.make_async_copy(
+            pack.at[side, :, pl.ds(ROWS - REACH, REACH)], land.at[side, :, pl.ds(EXT - REACH, REACH)], self_sem.at[side]
+        )
+
+    raw_low = rows_raw(last, to_low, 0, 5, N)
+    raw_fold = rows_raw(last, to_fold, 0, 0, N)
+    raw_high = rows_raw(first, to_high, 5, 0, S)
+    made_low = rows_made(last, to_low, 0, 5, N)
+    made_fold = rows_made(last, to_fold, 0, 0, N)
+    made_high = rows_made(first, to_high, 5, 0, S)
+    strips_low = [strip(0, ROWS - REACH, PAD - REACH, 10, 12, NA), strip(1, ROWS - REACH, PAD - REACH, 11, 13, NB)]
+    strips_fold = [strip(0, ROWS - REACH, EXT - REACH, 10, 10, NA), strip(1, ROWS - REACH, EXT - REACH, 11, 11, NB)]
+    strips_high = [strip(0, 0, PAD + ROWS, 12, 10, SA), strip(1, 0, PAD + ROWS, 13, 11, SB)]
+    strips_lon = [
+        send(pack.at[0], land.at[0, :, own], 14, 14, W),
+        send(pack.at[1], land.at[1, :, own], 15, 15, E),
+    ]
+
+    def start_all(copies):
+        for copy in copies:
+            copy.start()
+
+    def start_raw(link):
+        if link == N:
+            pl.when(inner)(lambda: start_all(raw_low))
+            pl.when(top)(lambda: start_all(raw_fold))
+        else:
+            start_all(raw_high)
+
+    def start_made(link):
+        if link in (W, E):
+            strips_lon[link - W].start()
+        elif link == N:
+            pl.when(inner)(lambda: made_low.start())
+            pl.when(top)(lambda: made_fold.start())
+        elif link in (NA, NB):
+            pl.when(inner)(lambda: strips_low[link - NA].start())
+            pl.when(top)(lambda: strips_fold[link - NA].start())
+        elif link == S:
+            made_high.start()
+        else:
+            strips_high[link - SA].start()
+
+    count = sum(jnp.where(g, 1, 0) for g in greeted)
+    pl.when(count > 0)(lambda: pl.semaphore_wait(barrier, count))
+    for link in range(8):
+
+        @pl.when(greeted[link])
+        def _(link=link):
+            pl.semaphore_signal(ready.at[reverse[link]], inc=1, device_id=partner[link], device_id_type=MESH)
+
+    for link in (N, S):
+        pl.when(greeted[link])(lambda link=link: start_raw(link))
+
     for copy in loads:
         copy.wait()
-
-    cover = mask_in[...].astype(jnp.float32)
-    ext[2, own] = 0.125 * (sig_in[0] + sig_in[1])
-    ext[3, own] = 0.125 * (sig_in[0] - sig_in[1])
-    ext[4, own] = 0.25 * sig_in[2]
-    ext[5, own] = (1.0 / 24.0) * cover * str_in[...]
-    ext[6, own] = cover * (1.0 / 1.5)
-    ext[7, own] = wind_in[0].astype(jnp.float32)
-    ext[8, own] = wind_in[1].astype(jnp.float32)
+    made[0] = mask_in[...].astype(jnp.float32)
+    made[1] = wind_in[0].astype(jnp.float32)
+    made[2] = wind_in[1].astype(jnp.float32)
+    block = [vel_in.at[0], vel_in.at[1], sig_in.at[0], sig_in.at[1], sig_in.at[2], str_in]
+    block += [made.at[0], made.at[1], made.at[2], cot_in.at[0], cot_in.at[1]]
 
     lanes = lane_ids((ROWS, COLS))
     for side in range(2):
         for plane in range(2):
             packed = None
             for field in range(NFLD):
-                at_plane, first, width = slot_of(field)
+                at_plane, begin_to, width = slot_of(field)
                 if at_plane != plane:
                     continue
                 begin = 0 if side == 0 else COLS - width
-                value = ext[field, own]
-                shift = (first - begin) % COLS
+                value = block[field][...]
+                shift = (begin_to - begin) % COLS
                 if shift:
                     value = pltpu.roll(value, shift, 1)
-                packed = value if packed is None else jnp.where(lanes < first, packed, value)
+                packed = value if packed is None else jnp.where(lanes < begin_to, packed, value)
             pack[side, plane] = packed
 
-    @pl.when(bottom)
+    for link in (N, S, NA, NB, SA, SB, W, E):
+        pl.when(greeted[link])(lambda link=link: start_made(link))
+
+    for side, is_self in ((0, self_a), (1, self_b)):
+        pl.when(is_self)(lambda side=side: self_strip(side).start())
+
+    for link in (W, E, N, NA, NB, S, SA, SB):
+
+        @pl.when(greets[link])
+        def _(link=link):
+            pl.semaphore_wait(ready.at[link], 1)
+            if link in (N, S):
+                start_raw(link)
+            start_made(link)
+
+    for copy in strips_lon:
+        copy.wait_recv()
+    for copy in raw_high + [made_high]:
+        copy.wait_recv()
+    for side, is_self in ((0, self_a), (1, self_b)):
+        pl.when(is_self)(lambda side=side: self_strip(side).wait())
+        pl.when(jnp.logical_not(is_self))(lambda side=side: strips_high[side].wait_recv())
+
+    @pl.when(has_south)
     def _():
-        ext[:, pl.ds(0, PAD)] = jnp.zeros((NFLD, PAD, COLS), jnp.float32)
-        land[:, :, pl.ds(0, PAD)] = jnp.zeros((2, 2, PAD, COLS), jnp.float32)
-
-    count = (
-        3
-        + jnp.where(self_a, 0, 1)
-        + jnp.where(self_b, 0, 1)
-        + jnp.where(bottom, 0, 3)
-    )
-    pl.semaphore_wait(barrier, count)
-
-    def send(src, dst, slot, sem, dev_lon, dev_lat):
-        return pltpu.make_async_remote_copy(
-            src_ref=src,
-            dst_ref=dst,
-            send_sem=send_sem.at[slot],
-            recv_sem=recv_sem.at[sem],
-            device_id=(dev_lon, dev_lat),
-            device_id_type=MESH,
-        )
-
-    main = pl.ds(0, NMAIN)
-    tail = pl.ds(NMAIN, 2)
-    def north_sends(row_main, row_tail, sem):
-        return (
-            send(ext.at[main, pl.ds(PAD + ROWS - REACH, REACH)], ext.at[main, pl.ds(row_main, REACH)], 0, sem, north_lon, up),
-            send(ext.at[tail, pl.ds(PAD + ROWS - BACK, BACK)], ext.at[tail, pl.ds(row_tail, BACK)], 1, sem + 1, north_lon, up),
-        )
-
-    def north_strip(side, row, sem, dev_lon):
-        return send(
-            pack.at[side, :, pl.ds(ROWS - REACH, REACH)], land.at[side, :, pl.ds(row, REACH)], 2 + side, sem, dev_lon, up
-        )
-
-    def north_self(side):
-        return pltpu.make_async_copy(
-            pack.at[side, :, pl.ds(ROWS - REACH, REACH)],
-            land.at[side, :, pl.ds(EXT - REACH, REACH)],
-            self_sem.at[side],
-        )
-
-    south_sends = (
-        send(ext.at[main, pl.ds(PAD, REACH)], ext.at[main, pl.ds(PAD + ROWS, REACH)], 4, 2, lon, down),
-        send(ext.at[tail, pl.ds(PAD, BACK)], ext.at[tail, pl.ds(PAD + ROWS, BACK)], 5, 3, lon, down),
-        send(pack.at[0, :, pl.ds(0, REACH)], land.at[0, :, pl.ds(PAD + ROWS, REACH)], 6, 4, west, down),
-        send(pack.at[1, :, pl.ds(0, REACH)], land.at[1, :, pl.ds(PAD + ROWS, REACH)], 7, 5, east, down),
-    )
-    lon_sends = (
-        send(pack.at[0], land.at[0, :, own], 8, 0, west, lat),
-        send(pack.at[1], land.at[1, :, own], 9, 1, east, lat),
-    )
-    low = north_sends(PAD - REACH, PAD - BACK, 6)
-    fold = north_sends(EXT - REACH, EXT - BACK, 2)
-    low_strips = (north_strip(0, PAD - REACH, 8, north_a), north_strip(1, PAD - REACH, 9, north_b))
-    fold_strips = (north_strip(0, EXT - REACH, 4, north_a), north_strip(1, EXT - REACH, 5, north_b))
-
-    @pl.when(jnp.logical_not(top))
-    def _():
-        for copy in low + low_strips:
-            copy.start()
-
-    @pl.when(top)
-    def _():
-        for copy in fold:
-            copy.start()
-        for side, is_self in ((0, self_a), (1, self_b)):
-            pl.when(is_self)(lambda side=side: north_self(side).start())
-            pl.when(jnp.logical_not(is_self))(lambda side=side: fold_strips[side].start())
-
-    @pl.when(jnp.logical_not(bottom))
-    def _():
-        for copy in south_sends:
-            copy.start()
-
-    for copy in lon_sends:
-        copy.start()
-
-    lon_sends[0].wait_recv()
-    lon_sends[1].wait_recv()
-    south_sends[0].wait_recv()
-    south_sends[1].wait_recv()
-    for side, is_self in ((0, self_a), (1, self_b)):
-        pl.when(is_self)(lambda side=side: north_self(side).wait())
-        pl.when(jnp.logical_not(is_self))(lambda side=side: south_sends[2 + side].wait_recv())
-
-    @pl.when(jnp.logical_not(bottom))
-    def _():
-        for copy in low + low_strips:
+        for copy in raw_low + [made_low] + strips_low:
             copy.wait_recv()
-        for copy in south_sends:
+        for copy in raw_high + [made_high] + strips_high:
             copy.wait_send()
 
-    for copy in low:
+    for copy in raw_low + [made_low]:
         copy.wait_send()
     for side, is_self in ((0, self_a), (1, self_b)):
-        pl.when(jnp.logical_not(is_self))(lambda side=side: low_strips[side].wait_send())
-    for copy in lon_sends:
+        pl.when(jnp.logical_not(is_self))(lambda side=side: strips_low[side].wait_send())
+    for copy in strips_lon:
         copy.wait_send()
 
 
 def gather_halos(lon_count, lat_count, *operands):
     f32 = jnp.float32
+    hbm = pl.BlockSpec(memory_space=pltpu.HBM)
     return pl.pallas_call(
         partial(gather_kernel, lon_count, lat_count),
         out_shape=(
             jax.ShapeDtypeStruct((NFLD, EXT, COLS), f32),
             jax.ShapeDtypeStruct((2, 2, EXT, COLS), f32),
         ),
-        in_specs=[pl.BlockSpec(memory_space=pl.ANY)] * 6,
-        out_specs=(
-            pl.BlockSpec(memory_space=pltpu.VMEM),
-            pl.BlockSpec(memory_space=pltpu.VMEM),
-        ),
+        in_specs=[hbm] * 6,
+        out_specs=(hbm, hbm),
         scratch_shapes=[
+            pltpu.VMEM((2, ROWS, COLS), jnp.bfloat16),
+            pltpu.VMEM((ROWS, COLS), jnp.int32),
+            pltpu.VMEM((2, ROWS, COLS), f32),
             pltpu.VMEM((3, ROWS, COLS), f32),
             pltpu.VMEM((ROWS, COLS), f32),
-            pltpu.VMEM((2, ROWS, COLS), jnp.bfloat16),
-            pltpu.VMEM((ROWS, COLS), jnp.int32),
+            pltpu.VMEM((2, ROWS, COLS), f32),
+            pltpu.VMEM((3, ROWS, COLS), f32),
             pltpu.VMEM((2, 2, ROWS, COLS), f32),
             pltpu.SemaphoreType.DMA((6,)),
-            pltpu.SemaphoreType.DMA((10,)),
-            pltpu.SemaphoreType.DMA((10,)),
+            pltpu.SemaphoreType.DMA((16,)),
+            pltpu.SemaphoreType.DMA((16,)),
             pltpu.SemaphoreType.DMA((2,)),
+            pltpu.SemaphoreType.REGULAR((8,)),
         ],
         compiler_params=pltpu.CompilerParams(
-            collective_id=0, has_side_effects=True, vmem_limit_bytes=32 * 1024 * 1024
+            collective_id=0, has_side_effects=True, vmem_limit_bytes=VMEM_LIMIT
         ),
     )(*operands)
 
@@ -285,6 +358,12 @@
 def evp_kernel(
     lat_count,
     start,
+    vel,
+    sig,
+    strength,
+    wind,
+    mask,
+    cot,
     ext,
     land,
     final_vel,
@@ -298,16 +377,19 @@
     strain,
     carry,
 ):
-    top = lax.axis_index("lat") == lat_count - 1
     band = lax.axis_index("lat")
+    top = band == lat_count - 1
+    bottom = band == 0
     shape = (TILE, COLS)
     lane = lane_ids(shape)
     first_lane = lane == 0
     last_lane = lane == COLS - 1
     west_half = lane < COLS // 2
 
+    wind_f32 = wind[...].astype(jnp.float32)
     for r in range(0, EXT, TILE):
         rows = pl.ds(r, TILE)
+        side = []
         for field in range(NFLD):
             plane, first, width = slot_of(field)
             a = land[0, plane, rows]
@@ -318,8 +400,27 @@
                 a = pltpu.roll(a, shift_a, 1)
             if shift_b:
                 b = pltpu.roll(b, shift_b, 1)
-            fld[field, 0, rows] = ext[field, rows]
-            fld[field, 1, rows] = jnp.where(west_half, a, b)
+            side.append(jnp.where(west_half, a, b))
+        if PAD <= r < PAD + ROWS:
+            mine = pl.ds(r - PAD, TILE)
+            main = [vel[0, mine], vel[1, mine], sig[0, mine], sig[1, mine], sig[2, mine], strength[mine]]
+            main += [mask[mine].astype(jnp.float32), wind_f32[0, r - PAD : r - PAD + TILE], wind_f32[1, r - PAD : r - PAD + TILE], cot[0, mine], cot[1, mine]]
+        else:
+            main = [ext[field, rows] for field in range(NFLD)]
+        if r < PAD:
+            main = [jnp.where(bottom, 0.0, x) for x in main]
+            side = [jnp.where(bottom, 0.0, x) for x in side]
+        for p, q in enumerate((main, side)):
+            cover = q[6] * (1.0 / 1.5)
+            q[2:7] = [
+                0.125 * (q[2] + q[3]),
+                0.125 * (q[2] - q[3]),
+                0.25 * q[4],
+                (1.0 / 16.0) * cover * q[5],
+                cover,
+            ]
+            for field in range(NFLD):
+                fld[field, p, rows] = q[field]
 
     @pl.when(top)
     def _():
@@ -485,7 +586,7 @@
                     vel_grad[1, pl.ds(r - PAD, TILE)] = gv
 
 
-def evp_and_adjoint(lat_count, start, ext, land):
+def evp_and_adjoint(lat_count, start, *operands):
     f32 = jnp.float32
     vmem = pl.BlockSpec(memory_space=pltpu.VMEM)
     return pl.pallas_call(
@@ -495,7 +596,7 @@
             jax.ShapeDtypeStruct((2, ROWS, COLS), f32),
             jax.ShapeDtypeStruct((3, ROWS, COLS), f32),
         ),
-        in_specs=[pl.BlockSpec(memory_space=pltpu.SMEM), vmem, vmem],
+        in_specs=[pl.BlockSpec(memory_space=pltpu.SMEM)] + [vmem] * 8,
         out_specs=(vmem, vmem, vmem),
         scratch_shapes=[
             pltpu.VMEM((NFLD, 2, EXT, COLS), f32),
@@ -506,15 +607,14 @@
             pltpu.VMEM((3, 2, EXT, COLS), f32),
             pltpu.VMEM((3, 2, EXT, COLS), f32),
         ],
-        compiler_params=pltpu.CompilerParams(vmem_limit_bytes=32 * 1024 * 1024),
-    )(start, ext, land)
+        compiler_params=pltpu.CompilerParams(vmem_limit_bytes=VMEM_LIMIT),
+    )(start, *operands)
 
 
 def shards(lon_count, lat_count, velocity, stress, strength, wind_stress, ice_mask, start_step, velocity_cotangent):
-    ext, land = gather_halos(
-        lon_count, lat_count, velocity, stress, strength, wind_stress, ice_mask, velocity_cotangent
-    )
-    return evp_and_adjoint(lat_count, start_step, ext, land)
+    block = (velocity, stress, strength, wind_stress, ice_mask, velocity_cotangent)
+    halos = gather_halos(lon_count, lat_count, *block)
+    return evp_and_adjoint(lat_count, start_step, *block, *halos)
 
 
 def solution(mesh):

time: 43.6 us -> 38.3 us (0.88)
  the two profiles are of different devices: /device:TPU:390 before, /device:TPU:455 now
where the time goes in v2:
time: 38.3 us; the launch traced here: 38.1 us
  Pallas kernels  36.8 us (96%)
  between operations  1.28 us (3%)
    pallas_call x1, Pallas kernels, gather_halos(): pl.pallas_call(partial(gather_kernel, lon_count, lat_count), out_shape=(j...  26.8 us
    pallas_call x1, Pallas kernels, evp_and_adjoint(): pl.pallas_call(partial(evp_kernel, lat_count), out_shape=(jax.ShapeDtypeS...  10 us

profile of v2, /device:TPU:455, one launch (start us, length us, event | category | flops | bytes accessed | tf_op | source)
XLA Modules:
  0.0 38.1 jit_solution(2468091524471704589)
XLA Ops:
  1.3 26.8 %shard_map.94 = (f32[11,96,128]{2,1,0:T(8,128)}, f32[2,2,96,128]{3,2,1,0:T(8,128)}) custom-call(f32[2,48,128]{2,1,0:T(8,128)} %vel.3, f32[3,48,128]{2,1,0:T(8,128)} %sig.3, f32[48,128]{1,0:T(8,128)} %strength.3, bf16[2,48,128]{2,1,0:T(8,128)(2,1)} %wind.3, s32[48,128]{1,0:T(8,128)} %mask.3, f32[2,48,128]{2,1,0:T(8,128)} %cot.3), custom_call_target="tpu_custom_call" | custom-call | tf_op jit(solution)/shard_map/pallas_call | solution.py:306
  28.1 10.0 %shard_map.95 = (f32[2,48,128]{2,1,0:T(8,128)}, f32[2,48,128]{2,1,0:T(8,128)}, f32[3,48,128]{2,1,0:T(8,128)}) custom-call(s32[1]{0:T(128)S(6)} %copy.10.start, f32[2,48,128]{2,1,0:T(8,128)} %vel.3, f32[3,48,128]{2,1,0:T(8,128)} %sig.3, f32[48,128]{1,0:T(8,128)} %strength.3, bf16[2,48,128]{2,1,0:T(8,128)(2,1)} %wind.3, s32[48,128]{1,0:T(8,128)} %mask.3, ...), custom_call_target="tpu_custom_call" | custom-call | tf_op jit(solution)/shard_map/pallas_call | solution.py:592

commit v3 on v2

--- a/solution.py
+++ b/solution.py
@@ -25,12 +25,45 @@
 ODD_FIELDS = (0, 1, 7, 8, 9, 10)
 
 
+NEAR = 8
+FAR = REACH - NEAR
+FAR_SLOT = REACH - NEAR - 1
+WIDE = ROWS + 2 * NEAR
+
+
 def slot_of(field):
     if field < 5:
         return 0, SLOT * field, SLOT
     if field < NMAIN:
         return 1, SLOT * (field - 5), SLOT
     return 1, 4 * SLOT + BACK * (field - NMAIN), BACK
+
+
+def far_slot_of(field):
+    if field < NMAIN:
+        return FAR_SLOT * field, FAR_SLOT
+    return FAR_SLOT * NMAIN + (BACK - NEAR) * (field - NMAIN), BACK - NEAR
+
+
+def strips(block, slots, side, shape):
+    lanes = lane_ids(shape)
+    packed = None
+    for value, (to, width) in zip(block, slots):
+        shift = (to - (0 if side == 0 else COLS - width)) % COLS
+        if shift:
+            value = pltpu.roll(value, shift, 1)
+        packed = value if packed is None else jnp.where(lanes < to, packed, value)
+    return packed
+
+
+def unstrip(west, east, to, width):
+    shift_a = (-to) % COLS
+    shift_b = (COLS - width - to) % COLS
+    if shift_a:
+        west = pltpu.roll(west, shift_a, 1)
+    if shift_b:
+        east = pltpu.roll(east, shift_b, 1)
+    return jnp.where(lane_ids(west.shape) < COLS // 2, west, east)
 
 
 def lane_ids(shape):
@@ -59,6 +92,7 @@
     cot,
     ext,
     land,
+    far,
     wind_in,
     mask_in,
     vel_in,
@@ -67,6 +101,7 @@
     cot_in,
     made,
     pack,
+    far_pack,
     local_sem,
     send_sem,
     recv_sem,
@@ -147,32 +182,23 @@
 
     def rows_raw(row_of, to_of, slot, sem, link):
         return [
-            send(vel.at[:, pl.ds(row_of(REACH), REACH)], ext.at[pl.ds(0, 2), pl.ds(to_of(REACH), REACH)], slot, sem, link),
-            send(
-                sig.at[:, pl.ds(row_of(REACH - 1), REACH - 1)],
-                ext.at[pl.ds(2, 3), pl.ds(to_of(REACH - 1), REACH - 1)],
-                slot + 1,
-                sem + 1,
-                link,
-            ),
-            send(
-                strength.at[pl.ds(row_of(REACH - 1), REACH - 1)],
-                ext.at[5, pl.ds(to_of(REACH - 1), REACH - 1)],
-                slot + 2,
-                sem + 2,
-                link,
-            ),
-            send(cot.at[:, pl.ds(row_of(BACK), BACK)], ext.at[pl.ds(NMAIN, 2), pl.ds(to_of(BACK), BACK)], slot + 3, sem + 3, link),
+            send(arg.at[index + (pl.ds(row_of(n), n),)], ext.at[to + (pl.ds(to_of(n), n),)], slot + i, sem + i, link)
+            for i, (arg, index, to, n) in enumerate(
+                (
+                    (vel, (slice(None),), (pl.ds(0, 2),), REACH),
+                    (sig, (slice(None),), (pl.ds(2, 3),), REACH - 1),
+                    (strength, (), (5,), REACH - 1),
+                    (cot, (slice(None),), (pl.ds(NMAIN, 2),), BACK),
+                )
+            )
         ]
 
     def rows_made(row_of, to_of, slot, sem, link):
-        return send(
-            made.at[:, pl.ds(row_of(REACH - 1), REACH - 1)],
-            ext.at[pl.ds(6, 3), pl.ds(to_of(REACH - 1), REACH - 1)],
-            slot + 4,
-            sem + 4,
-            link,
-        )
+        n, m = REACH - 1, REACH - 2
+        return [
+            send(made.at[0, pl.ds(row_of(n), n)], ext.at[6, pl.ds(to_of(n), n)], slot + 4, sem + 4, link),
+            send(made.at[pl.ds(1, 2), pl.ds(row_of(m), m)], ext.at[pl.ds(7, 2), pl.ds(to_of(m), m)], slot + 5, sem + 5, link),
+        ]
 
     last = lambda n: ROWS - n
     to_low = lambda n: PAD - n
@@ -180,52 +206,61 @@
     first = lambda n: 0
     to_high = lambda n: PAD + ROWS
 
-    def strip(side, row, to, slot, sem, link):
-        return send(pack.at[side, :, pl.ds(row, REACH)], land.at[side, :, pl.ds(to, REACH)], slot, sem, link)
-
-    def self_strip(side):
-        return pltpu.make_async_copy(
-            pack.at[side, :, pl.ds(ROWS - REACH, REACH)], land.at[side, :, pl.ds(EXT - REACH, REACH)], self_sem.at[side]
-        )
-
-    raw_low = rows_raw(last, to_low, 0, 5, N)
+    def corner(side, row, to, far_row, far_to, slot, sem, link):
+        return [
+            send(pack.at[side, :, pl.ds(row, NEAR)], land.at[side, :, pl.ds(to, NEAR)], slot, sem, link),
+            send(far_pack.at[side, pl.ds(far_row, FAR)], far.at[side, pl.ds(far_to, FAR)], slot + 1, sem + 1, link),
+        ]
+
+    def self_corner(side):
+        return [
+            pltpu.make_async_copy(
+                pack.at[side, :, pl.ds(ROWS - NEAR, NEAR)], land.at[side, :, pl.ds(NEAR + ROWS, NEAR)], self_sem.at[2 * side]
+            ),
+            pltpu.make_async_copy(
+                far_pack.at[side, pl.ds(ROWS - REACH, FAR)], far.at[side, pl.ds(PAD - NEAR + 2, FAR)], self_sem.at[2 * side + 1]
+            ),
+        ]
+
+    raw_low = rows_raw(last, to_low, 0, 6, N)
     raw_fold = rows_raw(last, to_fold, 0, 0, N)
-    raw_high = rows_raw(first, to_high, 5, 0, S)
-    made_low = rows_made(last, to_low, 0, 5, N)
+    raw_high = rows_raw(first, to_high, 6, 0, S)
+    made_low = rows_made(last, to_low, 0, 6, N)
     made_fold = rows_made(last, to_fold, 0, 0, N)
-    made_high = rows_made(first, to_high, 5, 0, S)
-    strips_low = [strip(0, ROWS - REACH, PAD - REACH, 10, 12, NA), strip(1, ROWS - REACH, PAD - REACH, 11, 13, NB)]
-    strips_fold = [strip(0, ROWS - REACH, EXT - REACH, 10, 10, NA), strip(1, ROWS - REACH, EXT - REACH, 11, 11, NB)]
-    strips_high = [strip(0, 0, PAD + ROWS, 12, 10, SA), strip(1, 0, PAD + ROWS, 13, 11, SB)]
+    made_high = rows_made(first, to_high, 6, 0, S)
+    far_low, far_high = PAD - REACH, PAD - NEAR
+    corners_low = [corner(i, ROWS - NEAR, 0, ROWS - REACH, far_low, 12 + 2 * i, 16 + 2 * i, NA + i) for i in range(2)]
+    corners_fold = [
+        corner(i, ROWS - NEAR, NEAR + ROWS, ROWS - REACH, far_high + 2, 12 + 2 * i, 12 + 2 * i, NA + i) for i in range(2)
+    ]
+    corners_high = [corner(i, 0, NEAR + ROWS, NEAR, far_high, 16 + 2 * i, 12 + 2 * i, SA + i) for i in range(2)]
     strips_lon = [
-        send(pack.at[0], land.at[0, :, own], 14, 14, W),
-        send(pack.at[1], land.at[1, :, own], 15, 15, E),
+        send(pack.at[0], land.at[0, :, pl.ds(NEAR, ROWS)], 20, 20, W),
+        send(pack.at[1], land.at[1, :, pl.ds(NEAR, ROWS)], 21, 21, E),
     ]
 
     def start_all(copies):
         for copy in copies:
             copy.start()
 
-    def start_raw(link):
+    def start_rows(link, part):
+        def pick(raw, made_rows):
+            return raw[:1] if part == 0 else raw[1:3] + made_rows + raw[3:]
+
         if link == N:
-            pl.when(inner)(lambda: start_all(raw_low))
-            pl.when(top)(lambda: start_all(raw_fold))
+            pl.when(inner)(lambda: start_all(pick(raw_low, made_low)))
+            pl.when(top)(lambda: start_all(pick(raw_fold, made_fold)))
         else:
-            start_all(raw_high)
-
-    def start_made(link):
+            start_all(pick(raw_high, made_high))
+
+    def start_strips(link):
         if link in (W, E):
             strips_lon[link - W].start()
-        elif link == N:
-            pl.when(inner)(lambda: made_low.start())
-            pl.when(top)(lambda: made_fold.start())
         elif link in (NA, NB):
-            pl.when(inner)(lambda: strips_low[link - NA].start())
-            pl.when(top)(lambda: strips_fold[link - NA].start())
-        elif link == S:
-            made_high.start()
+            pl.when(inner)(lambda: start_all(corners_low[link - NA]))
+            pl.when(top)(lambda: start_all(corners_fold[link - NA]))
         else:
-            strips_high[link - SA].start()
+            start_all(corners_high[link - SA])
 
     count = sum(jnp.where(g, 1, 0) for g in greeted)
     pl.when(count > 0)(lambda: pl.semaphore_wait(barrier, count))
@@ -236,7 +271,7 @@
             pl.semaphore_signal(ready.at[reverse[link]], inc=1, device_id=partner[link], device_id_type=MESH)
 
     for link in (N, S):
-        pl.when(greeted[link])(lambda link=link: start_raw(link))
+        pl.when(greeted[link])(lambda link=link: start_rows(link, 0))
 
     for copy in loads:
         copy.wait()
@@ -246,58 +281,69 @@
     block = [vel_in.at[0], vel_in.at[1], sig_in.at[0], sig_in.at[1], sig_in.at[2], str_in]
     block += [made.at[0], made.at[1], made.at[2], cot_in.at[0], cot_in.at[1]]
 
-    lanes = lane_ids((ROWS, COLS))
+    values = [ref[...] for ref in block]
     for side in range(2):
         for plane in range(2):
-            packed = None
-            for field in range(NFLD):
-                at_plane, begin_to, width = slot_of(field)
-                if at_plane != plane:
-                    continue
-                begin = 0 if side == 0 else COLS - width
-                value = block[field][...]
-                shift = (begin_to - begin) % COLS
-                if shift:
-                    value = pltpu.roll(value, shift, 1)
-                packed = value if packed is None else jnp.where(lanes < begin_to, packed, value)
-            pack[side, plane] = packed
-
-    for link in (N, S, NA, NB, SA, SB, W, E):
-        pl.when(greeted[link])(lambda link=link: start_made(link))
+            at = [f for f in range(NFLD) if slot_of(f)[0] == plane]
+            pack[side, plane] = strips([values[f] for f in at], [slot_of(f)[1:] for f in at], side, (ROWS, COLS))
+        inner_rows = slice(NEAR, ROWS - NEAR)
+        far_pack[side, NEAR : ROWS - NEAR] = strips(
+            [v[inner_rows] for v in values], [far_slot_of(f) for f in range(NFLD)], side, (ROWS - 2 * NEAR, COLS)
+        )
+
+    for link in (NA, NB, SA, SB, W, E):
+        pl.when(greeted[link])(lambda link=link: start_strips(link))
+    for link in (N, S):
+        pl.when(greeted[link])(lambda link=link: start_rows(link, 1))
 
     for side, is_self in ((0, self_a), (1, self_b)):
-        pl.when(is_self)(lambda side=side: self_strip(side).start())
-
-    for link in (W, E, N, NA, NB, S, SA, SB):
-
-        @pl.when(greets[link])
+        pl.when(is_self)(lambda side=side: start_all(self_corner(side)))
+
+    for link, when in (
+        [(link, always) for link in (W, E)]
+        + [(link, inner) for link in (N, NA, NB)]
+        + [(link, always) for link in (S, SA, SB)]
+        + [(link, top) for link in (N, NA, NB)]
+    ):
+
+        @pl.when(jnp.logical_and(greets[link], when))
         def _(link=link):
             pl.semaphore_wait(ready.at[link], 1)
             if link in (N, S):
-                start_raw(link)
-            start_made(link)
-
-    for copy in strips_lon:
-        copy.wait_recv()
-    for copy in raw_high + [made_high]:
-        copy.wait_recv()
+                start_rows(link, 0)
+                start_rows(link, 1)
+            else:
+                start_strips(link)
+
+    def received(copies):
+        for copy in copies:
+            copy.wait_recv()
+
+    def sent(copies):
+        for copy in copies:
+            copy.wait_send()
+
+    received(strips_lon)
+    received(raw_high + made_high)
     for side, is_self in ((0, self_a), (1, self_b)):
-        pl.when(is_self)(lambda side=side: self_strip(side).wait())
-        pl.when(jnp.logical_not(is_self))(lambda side=side: strips_high[side].wait_recv())
+
+        @pl.when(is_self)
+        def _(side=side):
+            for copy in self_corner(side):
+                copy.wait()
+
+        @pl.when(jnp.logical_not(is_self))
+        def _(side=side):
+            received(corners_high[side])
+            sent(corners_low[side])
 
     @pl.when(has_south)
     def _():
-        for copy in raw_low + [made_low] + strips_low:
-            copy.wait_recv()
-        for copy in raw_high + [made_high] + strips_high:
-            copy.wait_send()
-
-    for copy in raw_low + [made_low]:
-        copy.wait_send()
-    for side, is_self in ((0, self_a), (1, self_b)):
-        pl.when(jnp.logical_not(is_self))(lambda side=side: strips_low[side].wait_send())
-    for copy in strips_lon:
-        copy.wait_send()
+        received(raw_low + made_low + corners_low[0] + corners_low[1])
+        sent(raw_high + made_high + corners_high[0] + corners_high[1])
+
+    sent(raw_low + made_low)
+    sent(strips_lon)
 
 
 def gather_halos(lon_count, lat_count, *operands):
@@ -307,10 +353,11 @@
         partial(gather_kernel, lon_count, lat_count),
         out_shape=(
             jax.ShapeDtypeStruct((NFLD, EXT, COLS), f32),
-            jax.ShapeDtypeStruct((2, 2, EXT, COLS), f32),
+            jax.ShapeDtypeStruct((2, 2, WIDE, COLS), f32),
+            jax.ShapeDtypeStruct((2, 2 * (PAD - NEAR), COLS), f32),
         ),
         in_specs=[hbm] * 6,
-        out_specs=(hbm, hbm),
+        out_specs=(hbm, hbm, hbm),
         scratch_shapes=[
             pltpu.VMEM((2, ROWS, COLS), jnp.bfloat16),
             pltpu.VMEM((ROWS, COLS), jnp.int32),
@@ -320,10 +367,11 @@
             pltpu.VMEM((2, ROWS, COLS), f32),
             pltpu.VMEM((3, ROWS, COLS), f32),
             pltpu.VMEM((2, 2, ROWS, COLS), f32),
+            pltpu.VMEM((2, ROWS, COLS), f32),
             pltpu.SemaphoreType.DMA((6,)),
-            pltpu.SemaphoreType.DMA((16,)),
-            pltpu.SemaphoreType.DMA((16,)),
-            pltpu.SemaphoreType.DMA((2,)),
+            pltpu.SemaphoreType.DMA((22,)),
+            pltpu.SemaphoreType.DMA((22,)),
+            pltpu.SemaphoreType.DMA((4,)),
             pltpu.SemaphoreType.REGULAR((8,)),
         ],
         compiler_params=pltpu.CompilerParams(
@@ -342,17 +390,9 @@
 
 
 def flip_tile(value):
-    lane = lane_ids(value.shape)
-    bit = 1
-    while bit < COLS:
-        value = jnp.where((lane & bit) != 0, pltpu.roll(value, bit, 1), pltpu.roll(value, COLS - bit, 1))
-        bit *= 2
+    value = jnp.take_along_axis(value, COLS - 1 - lane_ids(value.shape), axis=1)
     row = lax.broadcasted_iota(jnp.int32, value.shape, 0)
-    bit = 1
-    while bit < TILE:
-        value = jnp.where((row & bit) != 0, pltpu.roll(value, bit, 0), pltpu.roll(value, TILE - bit, 0))
-        bit *= 2
-    return value
+    return jnp.take_along_axis(value, TILE - 1 - row, axis=0)
 
 
 def evp_kernel(
@@ -366,6 +406,7 @@
     cot,
     ext,
     land,
+    far,
     final_vel,
     vel_grad,
     sig_grad,
@@ -384,23 +425,20 @@
     lane = lane_ids(shape)
     first_lane = lane == 0
     last_lane = lane == COLS - 1
-    west_half = lane < COLS // 2
 
     wind_f32 = wind[...].astype(jnp.float32)
     for r in range(0, EXT, TILE):
         rows = pl.ds(r, TILE)
         side = []
         for field in range(NFLD):
-            plane, first, width = slot_of(field)
-            a = land[0, plane, rows]
-            b = land[1, plane, rows]
-            shift_a = (-first) % COLS
-            shift_b = (COLS - width - first) % COLS
-            if shift_a:
-                a = pltpu.roll(a, shift_a, 1)
-            if shift_b:
-                b = pltpu.roll(b, shift_b, 1)
-            side.append(jnp.where(west_half, a, b))
+            if PAD - NEAR <= r < PAD + ROWS + NEAR:
+                plane, to, width = slot_of(field)
+                near = pl.ds(r - PAD + NEAR, TILE)
+                side.append(unstrip(land[0, plane, near], land[1, plane, near], to, width))
+            else:
+                to, width = far_slot_of(field)
+                beyond = pl.ds(r if r < PAD else r - ROWS - 2 * NEAR, TILE)
+                side.append(unstrip(far[0, beyond], far[1, beyond], to, width))
         if PAD <= r < PAD + ROWS:
             mine = pl.ds(r - PAD, TILE)
             main = [vel[0, mine], vel[1, mine], sig[0, mine], sig[1, mine], sig[2, mine], strength[mine]]
@@ -429,8 +467,9 @@
             sign = jnp.where(odd, -1.0, 1.0)
             for plane in range(2):
                 old = [fld[i, plane, pl.ds(PAD + ROWS + t * TILE, TILE)] for t in range(3)]
+                order = (2, 1, 0) if plane == 0 else (0, 2, 1)
                 for t in range(3):
-                    fld[i, plane, pl.ds(PAD + ROWS + t * TILE, TILE)] = sign * flip_tile(old[2 - t])
+                    fld[i, plane, pl.ds(PAD + ROWS + t * TILE, TILE)] = sign * flip_tile(old[order[t]])
             return 0
 
         lax.fori_loop(0, NFLD, one, 0)
@@ -596,7 +635,7 @@
             jax.ShapeDtypeStruct((2, ROWS, COLS), f32),
             jax.ShapeDtypeStruct((3, ROWS, COLS), f32),
         ),
-        in_specs=[pl.BlockSpec(memory_space=pltpu.SMEM)] + [vmem] * 8,
+        in_specs=[pl.BlockSpec(memory_space=pltpu.SMEM)] + [vmem] * 9,
         out_specs=(vmem, vmem, vmem),
         scratch_shapes=[
             pltpu.VMEM((NFLD, 2, EXT, COLS), f32),

time: 38.3 us -> 33.6 us (0.88)
  the two profiles are of different devices: /device:TPU:455 before, /device:TPU:415 now
where the time goes in v3:
time: 33.6 us; the launch traced here: 33.4 us
  Pallas kernels  32.1 us (96%)
  between operations  1.28 us (4%)
    pallas_call x1, Pallas kernels, gather_halos(): pl.pallas_call(partial(gather_kernel, lon_count, lat_count), out_shape=(j...  26.6 us
    pallas_call x1, Pallas kernels, evp_and_adjoint(): pl.pallas_call(partial(evp_kernel, lat_count), out_shape=(jax.ShapeDtypeS...  5.45 us

profile of v3, /device:TPU:415, one launch (start us, length us, event | category | flops | bytes accessed | tf_op | source)
XLA Modules:
  0.0 33.4 jit_solution(14378969400440992237)
XLA Ops:
  1.3 26.6 %shard_map.94 = (f32[11,96,128]{2,1,0:T(8,128)}, f32[2,2,64,128]{3,2,1,0:T(8,128)}, f32[2,32,128]{2,1,0:T(8,128)}) custom-call(f32[2,48,128]{2,1,0:T(8,128)} %vel.3, f32[3,48,128]{2,1,0:T(8,128)} %sig.3, f32[48,128]{1,0:T(8,128)} %strength.3, bf16[2,48,128]{2,1,0:T(8,128)(2,1)} %wind.3, s32[48,128]{1,0:T(8,128)} %mask.3, f32[2,48,128]{2,1,0:T(8,128)} %cot.3), custom_call_target="tpu_custom_call" | custom-call | tf_op jit(solution)/shard_map/pallas_call | solution.py:352
  27.9 5.5 %shard_map.95 = (f32[2,48,128]{2,1,0:T(8,128)}, f32[2,48,128]{2,1,0:T(8,128)}, f32[3,48,128]{2,1,0:T(8,128)}) custom-call(s32[1]{0:T(128)S(6)} %copy.10.start, f32[2,48,128]{2,1,0:T(8,128)} %vel.3, f32[3,48,128]{2,1,0:T(8,128)} %sig.3, f32[48,128]{1,0:T(8,128)} %strength.3, bf16[2,48,128]{2,1,0:T(8,128)(2,1)} %wind.3, s32[48,128]{1,0:T(8,128)} %mask.3, ...), custom_call_target="tpu_custom_call" | custom-call | tf_op jit(solution)/shard_map/pallas_call | solution.py:631

commit v4 on v3

--- a/solution.py
+++ b/solution.py
@@ -10,7 +10,7 @@
 NSUB = 6
 EVP_TOTAL = 120
 MESH = pl.DeviceIdType.MESH
-VMEM_LIMIT = 60 * 1024 * 1024
+VMEM_LIMIT = 32 * 1024 * 1024
 
 ROWS = 48
 COLS = 128
@@ -26,7 +26,7 @@
 
 
 NEAR = 8
-FAR = REACH - NEAR
+FAR = REACH - NEAR - 1
 FAR_SLOT = REACH - NEAR - 1
 WIDE = ROWS + 2 * NEAR
 
@@ -70,11 +70,15 @@
     return lax.broadcasted_iota(jnp.int32, shape, len(shape) - 1)
 
 
+def digit(value, size, count):
+    return sum(jnp.where(value >= size * i, 1, 0) for i in range(1, count))
+
+
 def start_order(lon, lat):
-    y = lax.div(lon, 8)
-    z_low = lax.rem(lax.div(lon, 2), 4)
-    x = lax.div(lat, 4)
-    z_high = lax.rem(lat, 4)
+    y = digit(lon, 8, 4)
+    z_low = digit(lon - 8 * y, 2, 4)
+    x = digit(lat, 4, 4)
+    z_high = lat - 4 * x
     early_half = z_high < 2
     base = jnp.where(early_half, 44 * z_high, 96 - 4 * z_high)
     step = jnp.where(early_half, 13, 4)
@@ -97,7 +101,6 @@
     mask_in,
     vel_in,
     sig_in,
-    str_in,
     cot_in,
     made,
     pack,
@@ -113,13 +116,13 @@
     top = lat == lat_count - 1
     inner = jnp.logical_not(top)
     has_south = lat > 0
-    west = lax.rem(lon + lon_count - 1, lon_count)
-    east = lax.rem(lon + 1, lon_count)
+    west = jnp.where(lon == 0, lon_count - 1, lon - 1)
+    east = jnp.where(lon == lon_count - 1, 0, lon + 1)
     up = jnp.where(top, lat, lat + 1)
     down = jnp.where(has_south, lat - 1, lat)
     north_lon = jnp.where(top, lon_count - 1 - lon, lon)
-    north_a = jnp.where(top, lax.rem(lon_count - lon, lon_count), west)
-    north_b = jnp.where(top, lax.rem(2 * lon_count - 2 - lon, lon_count), east)
+    north_a = jnp.where(top, jnp.where(lon == 0, 0, lon_count - lon), west)
+    north_b = jnp.where(top, lon_count - 2 - lon + jnp.where(lon == lon_count - 1, lon_count, 0), east)
     self_a = jnp.logical_and(top, north_a == lon)
     self_b = jnp.logical_and(top, north_b == lon)
     always = lat >= 0
@@ -147,9 +150,13 @@
         NA,
     ]
     mine = start_order(lon, lat)
-    later = [start_order(*p) > mine for p in partner]
-    greets = [jnp.logical_and(t, l) for t, l in zip(there, later)]
-    greeted = [jnp.logical_and(t, jnp.logical_not(l)) for t, l in zip(there, later)]
+    plain = [(west, lat), (east, lat), (lon, up), (west, up), (east, up), (lon, down), (west, down), (east, down)]
+    later = [start_order(*p) > mine for p in plain]
+    folded = [jnp.logical_and(top, link in (N, NA, NB)) for link in range(8)]
+    answers = [there[i] & jnp.logical_not(later[i]) & jnp.logical_not(folded[i]) for i in range(8)]
+    awaits = [there[i] & later[i] & jnp.logical_not(folded[i]) for i in range(8)]
+    greets = [there[i] & (later[i] | folded[i]) for i in range(8)]
+    greeted = [there[i] & (jnp.logical_not(later[i]) | folded[i]) for i in range(8)]
 
     barrier = pltpu.get_barrier_semaphore()
     for link in range(8):
@@ -164,7 +171,7 @@
         pltpu.make_async_copy(mask, mask_in, local_sem.at[1]),
         pltpu.make_async_copy(vel, vel_in, local_sem.at[2]),
         pltpu.make_async_copy(sig, sig_in, local_sem.at[3]),
-        pltpu.make_async_copy(strength, str_in, local_sem.at[4]),
+        pltpu.make_async_copy(strength, made.at[0], local_sem.at[4]),
         pltpu.make_async_copy(cot, cot_in, local_sem.at[5]),
     ]
     for copy in loads:
@@ -187,7 +194,6 @@
                 (
                     (vel, (slice(None),), (pl.ds(0, 2),), REACH),
                     (sig, (slice(None),), (pl.ds(2, 3),), REACH - 1),
-                    (strength, (), (5,), REACH - 1),
                     (cot, (slice(None),), (pl.ds(NMAIN, 2),), BACK),
                 )
             )
@@ -196,8 +202,8 @@
     def rows_made(row_of, to_of, slot, sem, link):
         n, m = REACH - 1, REACH - 2
         return [
-            send(made.at[0, pl.ds(row_of(n), n)], ext.at[6, pl.ds(to_of(n), n)], slot + 4, sem + 4, link),
-            send(made.at[pl.ds(1, 2), pl.ds(row_of(m), m)], ext.at[pl.ds(7, 2), pl.ds(to_of(m), m)], slot + 5, sem + 5, link),
+            send(made.at[pl.ds(0, 2), pl.ds(row_of(n), n)], ext.at[pl.ds(5, 2), pl.ds(to_of(n), n)], slot + 3, sem + 3, link),
+            send(made.at[pl.ds(2, 2), pl.ds(row_of(m), m)], ext.at[pl.ds(7, 2), pl.ds(to_of(m), m)], slot + 4, sem + 4, link),
         ]
 
     last = lambda n: ROWS - n
@@ -218,7 +224,7 @@
                 pack.at[side, :, pl.ds(ROWS - NEAR, NEAR)], land.at[side, :, pl.ds(NEAR + ROWS, NEAR)], self_sem.at[2 * side]
             ),
             pltpu.make_async_copy(
-                far_pack.at[side, pl.ds(ROWS - REACH, FAR)], far.at[side, pl.ds(PAD - NEAR + 2, FAR)], self_sem.at[2 * side + 1]
+                far_pack.at[side, pl.ds(ROWS - REACH + 1, FAR)], far.at[side, pl.ds(PAD - NEAR + 3, FAR)], self_sem.at[2 * side + 1]
             ),
         ]
 
@@ -228,10 +234,11 @@
     made_low = rows_made(last, to_low, 0, 6, N)
     made_fold = rows_made(last, to_fold, 0, 0, N)
     made_high = rows_made(first, to_high, 6, 0, S)
-    far_low, far_high = PAD - REACH, PAD - NEAR
-    corners_low = [corner(i, ROWS - NEAR, 0, ROWS - REACH, far_low, 12 + 2 * i, 16 + 2 * i, NA + i) for i in range(2)]
+    far_low, far_high = PAD - REACH + 1, PAD - NEAR
+    far_row = ROWS - REACH + 1
+    corners_low = [corner(i, ROWS - NEAR, 0, far_row, far_low, 12 + 2 * i, 16 + 2 * i, NA + i) for i in range(2)]
     corners_fold = [
-        corner(i, ROWS - NEAR, NEAR + ROWS, ROWS - REACH, far_high + 2, 12 + 2 * i, 12 + 2 * i, NA + i) for i in range(2)
+        corner(i, ROWS - NEAR, NEAR + ROWS, far_row, far_high + 3, 12 + 2 * i, 12 + 2 * i, NA + i) for i in range(2)
     ]
     corners_high = [corner(i, 0, NEAR + ROWS, NEAR, far_high, 16 + 2 * i, 12 + 2 * i, SA + i) for i in range(2)]
     strips_lon = [
@@ -245,7 +252,7 @@
 
     def start_rows(link, part):
         def pick(raw, made_rows):
-            return raw[:1] if part == 0 else raw[1:3] + made_rows + raw[3:]
+            return (raw[:1], raw[1:2], made_rows + raw[2:])[part]
 
         if link == N:
             pl.when(inner)(lambda: start_all(pick(raw_low, made_low)))
@@ -266,7 +273,7 @@
     pl.when(count > 0)(lambda: pl.semaphore_wait(barrier, count))
     for link in range(8):
 
-        @pl.when(greeted[link])
+        @pl.when(answers[link])
         def _(link=link):
             pl.semaphore_signal(ready.at[reverse[link]], inc=1, device_id=partner[link], device_id_type=MESH)
 
@@ -275,11 +282,11 @@
 
     for copy in loads:
         copy.wait()
-    made[0] = mask_in[...].astype(jnp.float32)
-    made[1] = wind_in[0].astype(jnp.float32)
-    made[2] = wind_in[1].astype(jnp.float32)
-    block = [vel_in.at[0], vel_in.at[1], sig_in.at[0], sig_in.at[1], sig_in.at[2], str_in]
-    block += [made.at[0], made.at[1], made.at[2], cot_in.at[0], cot_in.at[1]]
+    made[1] = mask_in[...].astype(jnp.float32)
+    made[2] = wind_in[0].astype(jnp.float32)
+    made[3] = wind_in[1].astype(jnp.float32)
+    block = [vel_in.at[0], vel_in.at[1], sig_in.at[0], sig_in.at[1], sig_in.at[2]]
+    block += [made.at[0], made.at[1], made.at[2], made.at[3], cot_in.at[0], cot_in.at[1]]
 
     values = [ref[...] for ref in block]
     for side in range(2):
@@ -293,27 +300,29 @@
 
     for link in (NA, NB, SA, SB, W, E):
         pl.when(greeted[link])(lambda link=link: start_strips(link))
-    for link in (N, S):
-        pl.when(greeted[link])(lambda link=link: start_rows(link, 1))
+    patient = top & (lon < lon_count // 2)
+    for part in (1, 2):
+        for link in (N, S):
+            wait = patient if link == N else jnp.logical_not(always)
+            pl.when(greeted[link] & jnp.logical_not(wait))(lambda link=link, part=part: start_rows(link, part))
 
     for side, is_self in ((0, self_a), (1, self_b)):
         pl.when(is_self)(lambda side=side: start_all(self_corner(side)))
 
-    for link, when in (
-        [(link, always) for link in (W, E)]
-        + [(link, inner) for link in (N, NA, NB)]
-        + [(link, always) for link in (S, SA, SB)]
-        + [(link, top) for link in (N, NA, NB)]
-    ):
-
-        @pl.when(jnp.logical_and(greets[link], when))
+    for link in (W, E, N, NA, NB, S, SA, SB):
+
+        @pl.when(awaits[link])
         def _(link=link):
             pl.semaphore_wait(ready.at[link], 1)
             if link in (N, S):
                 start_rows(link, 0)
                 start_rows(link, 1)
+                start_rows(link, 2)
             else:
                 start_strips(link)
+
+    for part in (1, 2):
+        pl.when(patient)(lambda part=part: start_rows(N, part))
 
     def received(copies):
         for copy in copies:
@@ -348,7 +357,7 @@
 
 def gather_halos(lon_count, lat_count, *operands):
     f32 = jnp.float32
-    hbm = pl.BlockSpec(memory_space=pltpu.HBM)
+    anywhere = pl.BlockSpec(memory_space=pl.ANY)
     return pl.pallas_call(
         partial(gather_kernel, lon_count, lat_count),
         out_shape=(
@@ -356,16 +365,15 @@
             jax.ShapeDtypeStruct((2, 2, WIDE, COLS), f32),
             jax.ShapeDtypeStruct((2, 2 * (PAD - NEAR), COLS), f32),
         ),
-        in_specs=[hbm] * 6,
-        out_specs=(hbm, hbm, hbm),
+        in_specs=[pl.BlockSpec(memory_space=pltpu.HBM)] * 6,
+        out_specs=(anywhere, anywhere, anywhere),
         scratch_shapes=[
             pltpu.VMEM((2, ROWS, COLS), jnp.bfloat16),
             pltpu.VMEM((ROWS, COLS), jnp.int32),
             pltpu.VMEM((2, ROWS, COLS), f32),
             pltpu.VMEM((3, ROWS, COLS), f32),
-            pltpu.VMEM((ROWS, COLS), f32),
             pltpu.VMEM((2, ROWS, COLS), f32),
-            pltpu.VMEM((3, ROWS, COLS), f32),
+            pltpu.VMEM((4, ROWS, COLS), f32),
             pltpu.VMEM((2, 2, ROWS, COLS), f32),
             pltpu.VMEM((2, ROWS, COLS), f32),
             pltpu.SemaphoreType.DMA((6,)),
@@ -462,17 +470,13 @@
 
     @pl.when(top)
     def _():
-        def one(i, _):
-            odd = (i < 2) | (i >= 7)
-            sign = jnp.where(odd, -1.0, 1.0)
+        for field in range(NFLD):
             for plane in range(2):
-                old = [fld[i, plane, pl.ds(PAD + ROWS + t * TILE, TILE)] for t in range(3)]
+                old = [fld[field, plane, pl.ds(PAD + ROWS + t * TILE, TILE)] for t in range(3)]
                 order = (2, 1, 0) if plane == 0 else (0, 2, 1)
                 for t in range(3):
-                    fld[i, plane, pl.ds(PAD + ROWS + t * TILE, TILE)] = sign * flip_tile(old[order[t]])
-            return 0
-
-        lax.fori_loop(0, NFLD, one, 0)
+                    new = flip_tile(old[order[t]])
+                    fld[field, plane, pl.ds(PAD + ROWS + t * TILE, TILE)] = -new if field in ODD_FIELDS else new
 
     for r in range(0, EXT, TILE):
         rows = pl.ds(r, TILE)
@@ -652,7 +656,7 @@
 
 def shards(lon_count, lat_count, velocity, stress, strength, wind_stress, ice_mask, start_step, velocity_cotangent):
     block = (velocity, stress, strength, wind_stress, ice_mask, velocity_cotangent)
-    halos = gather_halos(lon_count, lat_count, *block)
+    halos = gather_halos(lon_count, lat_count, *(pltpu.with_memory_space_constraint(x, pltpu.HBM) for x in block))
     return evp_and_adjoint(lat_count, start_step, *block, *halos)
 
 

time: 33.6 us -> 31.3 us (0.932)
  the two profiles are of different devices: /device:TPU:415 before, /device:TPU:6 now
where the time goes in v4:
time: 31.3 us; the launch traced here: 30.8 us
  Pallas kernels  29.4 us (94%)
  between operations  1.38 us (4%)
    pallas_call x1, Pallas kernels, gather_halos(): pl.pallas_call(partial(gather_kernel, lon_count, lat_count), out_shape=(j...  26.1 us
    pallas_call x1, Pallas kernels, evp_and_adjoint(): pl.pallas_call(partial(evp_kernel, lat_count), out_shape=(jax.ShapeDtypeS...  3.32 us

profile of v4, /device:TPU:6, one launch (start us, length us, event | category | flops | bytes accessed | tf_op | source)
XLA Modules:
  0.0 30.8 jit_solution(15941402203758330551)
XLA Ops:
  1.3 0.0 copy-start
  1.3 0.0 copy-start.1
  1.3 0.0 copy-start.2
  1.3 0.0 copy-start.3
  1.3 0.0 copy-start.4
  1.3 0.0 copy-start.5
  1.3 26.1 %shard_map.94 = (f32[11,96,128]{2,1,0:T(8,128)S(1)}, f32[2,2,64,128]{3,2,1,0:T(8,128)S(1)}, f32[2,32,128]{2,1,0:T(8,128)S(1)}) custom-call(f32[2,48,128]{2,1,0:T(8,128)} %vel.3, f32[3,48,128]{2,1,0:T(8,128)} %sig.3, f32[48,128]{1,0:T(8,128)} %strength.3, bf16[2,48,128]{2,1,0:T(8,128)(2,1)} %wind.3, s32[48,128]{1,0:T(8,128)} %mask.3, f32[2,48,128]{2,1,0:T(8,128)} %cot.3), custom_call_target="tpu_custom_call" | custom-call | tf_op jit(solution)/shard_map/pallas_call | solution.py:361
  27.5 0.0 copy-done
  27.5 0.0 copy-done.1
  27.5 0.0 copy-done.2
  27.5 0.0 copy-done.3
  27.5 0.0 copy-done.4
  27.5 0.0 copy-done.5
  27.5 3.3 %shard_map.95 = (f32[2,48,128]{2,1,0:T(8,128)}, f32[2,48,128]{2,1,0:T(8,128)}, f32[3,48,128]{2,1,0:T(8,128)}) custom-call(s32[1]{0:T(128)S(6)} %copy.10.start, f32[2,48,128]{2,1,0:T(8,128)S(1)} %copy-done.1, f32[3,48,128]{2,1,0:T(8,128)S(1)} %copy-done, f32[48,128]{1,0:T(8,128)S(1)} %copy-done.3, bf16[2,48,128]{2,1,0:T(8,128)(2,1)S(1)} %copy-done.4, ...), custom_call_target="tpu_custom_call" | custom-call | tf_op jit(solution)/shard_map/pallas_call | solution.py:635
Async XLA Ops:
  1.3 26.2 %copy-start = (f32[3,48,128]{2,1,0:T(8,128)S(1)}, f32[3,48,128]{2,1,0:T(8,128)}, u32[]{:S(2)}) copy-start(f32[3,48,128]{2,1,0:T(8,128)} %sig.3) | copy-start | bytes 221188
  1.3 26.2 %copy-start.1 = (f32[2,48,128]{2,1,0:T(8,128)S(1)}, f32[2,48,128]{2,1,0:T(8,128)}, u32[]{:S(2)}) copy-start(f32[2,48,128]{2,1,0:T(8,128)} %vel.3) | copy-start | bytes 147460
  1.3 26.2 %copy-start.2 = (f32[2,48,128]{2,1,0:T(8,128)S(1)}, f32[2,48,128]{2,1,0:T(8,128)}, u32[]{:S(2)}) copy-start(f32[2,48,128]{2,1,0:T(8,128)} %cot.3) | copy-start | bytes 147460
  1.3 26.2 %copy-start.3 = (f32[48,128]{1,0:T(8,128)S(1)}, f32[48,128]{1,0:T(8,128)}, u32[]{:S(2)}) copy-start(f32[48,128]{1,0:T(8,128)} %strength.3) | copy-start | bytes 73732
  1.3 26.2 %copy-start.4 = (bf16[2,48,128]{2,1,0:T(8,128)(2,1)S(1)}, bf16[2,48,128]{2,1,0:T(8,128)(2,1)}, u32[]{:S(2)}) copy-start(bf16[2,48,128]{2,1,0:T(8,128)(2,1)} %wind.3) | copy-start | bytes 73732
  1.3 26.2 %copy-start.5 = (s32[48,128]{1,0:T(8,128)S(1)}, s32[48,128]{1,0:T(8,128)}, u32[]{:S(2)}) copy-start(s32[48,128]{1,0:T(8,128)} %mask.3) | copy-start | bytes 73732

commit v5 on v4

--- a/solution.py
+++ b/solution.py
@@ -18,6 +18,7 @@
 EXT = ROWS + 2 * PAD
 REACH = 22
 BACK = 12
+TILE = 8
 NFLD = 11
 NMAIN = 9
 SLOT = 24
@@ -25,10 +26,7 @@
 ODD_FIELDS = (0, 1, 7, 8, 9, 10)
 
 
-NEAR = 8
-FAR = REACH - NEAR - 1
-FAR_SLOT = REACH - NEAR - 1
-WIDE = ROWS + 2 * NEAR
+GROUP = 7
 
 
 def slot_of(field):
@@ -39,10 +37,28 @@
     return 1, 4 * SLOT + BACK * (field - NMAIN), BACK
 
 
-def far_slot_of(field):
-    if field < NMAIN:
-        return FAR_SLOT * field, FAR_SLOT
-    return FAR_SLOT * NMAIN + (BACK - NEAR) * (field - NMAIN), BACK - NEAR
+def corner_width(field, row):
+    return (REACH, REACH, *(REACH - 1,) * 5, REACH - 2, REACH - 2, BACK, BACK)[field] - row
+
+
+def corner_slots():
+    wide = [(0, field, corner_width(field, 1)) for field in range(NFLD)]
+    narrow = [(2, field, corner_width(field, 15)) for field in range(NMAIN)]
+    planes = [wide[:6] + narrow[2:3], wide[6:] + narrow[:2] + narrow[3:]]
+    planes.append([(1, field, corner_width(field, 8)) for field in range(NFLD)])
+    placed = []
+    for plane in planes:
+        to = 0
+        placed.append([])
+        for group, field, width in plane:
+            placed[-1].append((group, field, to, width))
+            to += width
+        assert to <= COLS
+    return placed
+
+
+def corner_rows(end, group):
+    return ROWS - TILE - GROUP * group if end == 0 else GROUP * group
 
 
 def strips(block, slots, side, shape):
@@ -96,7 +112,7 @@
     cot,
     ext,
     land,
-    far,
+    corners,
     wind_in,
     mask_in,
     vel_in,
@@ -104,7 +120,7 @@
     cot_in,
     made,
     pack,
-    far_pack,
+    corner_pack,
     local_sem,
     send_sem,
     recv_sem,
@@ -212,39 +228,26 @@
     first = lambda n: 0
     to_high = lambda n: PAD + ROWS
 
-    def corner(side, row, to, far_row, far_to, slot, sem, link):
-        return [
-            send(pack.at[side, :, pl.ds(row, NEAR)], land.at[side, :, pl.ds(to, NEAR)], slot, sem, link),
-            send(far_pack.at[side, pl.ds(far_row, FAR)], far.at[side, pl.ds(far_to, FAR)], slot + 1, sem + 1, link),
-        ]
+    seven = (pl.ds(1, GROUP), pl.ds(0, GROUP))
+
+    def corner(side, end, to, slot, sem, link):
+        return send(corner_pack.at[side, end, :, seven[end]], corners.at[side, to, :, seven[end]], slot, sem, link)
 
     def self_corner(side):
-        return [
-            pltpu.make_async_copy(
-                pack.at[side, :, pl.ds(ROWS - NEAR, NEAR)], land.at[side, :, pl.ds(NEAR + ROWS, NEAR)], self_sem.at[2 * side]
-            ),
-            pltpu.make_async_copy(
-                far_pack.at[side, pl.ds(ROWS - REACH + 1, FAR)], far.at[side, pl.ds(PAD - NEAR + 3, FAR)], self_sem.at[2 * side + 1]
-            ),
-        ]
-
-    raw_low = rows_raw(last, to_low, 0, 6, N)
+        return pltpu.make_async_copy(
+            corner_pack.at[side, 0, :, seven[0]], corners.at[side, 0, :, seven[0]], self_sem.at[side]
+        )
+
+    raw_low = rows_raw(last, to_low, 0, 5, N)
     raw_fold = rows_raw(last, to_fold, 0, 0, N)
-    raw_high = rows_raw(first, to_high, 6, 0, S)
-    made_low = rows_made(last, to_low, 0, 6, N)
+    raw_high = rows_raw(first, to_high, 5, 0, S)
+    made_low = rows_made(last, to_low, 0, 5, N)
     made_fold = rows_made(last, to_fold, 0, 0, N)
-    made_high = rows_made(first, to_high, 6, 0, S)
-    far_low, far_high = PAD - REACH + 1, PAD - NEAR
-    far_row = ROWS - REACH + 1
-    corners_low = [corner(i, ROWS - NEAR, 0, far_row, far_low, 12 + 2 * i, 16 + 2 * i, NA + i) for i in range(2)]
-    corners_fold = [
-        corner(i, ROWS - NEAR, NEAR + ROWS, far_row, far_high + 3, 12 + 2 * i, 12 + 2 * i, NA + i) for i in range(2)
-    ]
-    corners_high = [corner(i, 0, NEAR + ROWS, NEAR, far_high, 16 + 2 * i, 12 + 2 * i, SA + i) for i in range(2)]
-    strips_lon = [
-        send(pack.at[0], land.at[0, :, pl.ds(NEAR, ROWS)], 20, 20, W),
-        send(pack.at[1], land.at[1, :, pl.ds(NEAR, ROWS)], 21, 21, E),
-    ]
+    made_high = rows_made(first, to_high, 5, 0, S)
+    corners_low = [corner(i, 0, 1, 10 + i, 12 + i, NA + i) for i in range(2)]
+    corners_fold = [corner(i, 0, 0, 10 + i, 10 + i, NA + i) for i in range(2)]
+    corners_high = [corner(i, 1, 0, 12 + i, 10 + i, SA + i) for i in range(2)]
+    strips_lon = [send(pack.at[0], land.at[0], 14, 14, W), send(pack.at[1], land.at[1], 15, 15, E)]
 
     def start_all(copies):
         for copy in copies:
@@ -264,10 +267,10 @@
         if link in (W, E):
             strips_lon[link - W].start()
         elif link in (NA, NB):
-            pl.when(inner)(lambda: start_all(corners_low[link - NA]))
-            pl.when(top)(lambda: start_all(corners_fold[link - NA]))
+            pl.when(inner)(lambda: corners_low[link - NA].start())
+            pl.when(top)(lambda: corners_fold[link - NA].start())
         else:
-            start_all(corners_high[link - SA])
+            corners_high[link - SA].start()
 
     count = sum(jnp.where(g, 1, 0) for g in greeted)
     pl.when(count > 0)(lambda: pl.semaphore_wait(barrier, count))
@@ -293,10 +296,10 @@
         for plane in range(2):
             at = [f for f in range(NFLD) if slot_of(f)[0] == plane]
             pack[side, plane] = strips([values[f] for f in at], [slot_of(f)[1:] for f in at], side, (ROWS, COLS))
-        inner_rows = slice(NEAR, ROWS - NEAR)
-        far_pack[side, NEAR : ROWS - NEAR] = strips(
-            [v[inner_rows] for v in values], [far_slot_of(f) for f in range(NFLD)], side, (ROWS - 2 * NEAR, COLS)
-        )
+        for end in range(2):
+            for plane, slots in enumerate(corner_slots()):
+                parts = [block[field][pl.ds(corner_rows(end, group), TILE)] for group, field, _, _ in slots]
+                corner_pack[side, end, plane] = strips(parts, [slot[2:] for slot in slots], side, (TILE, COLS))
 
     for link in (NA, NB, SA, SB, W, E):
         pl.when(greeted[link])(lambda link=link: start_strips(link))
@@ -307,7 +310,7 @@
             pl.when(greeted[link] & jnp.logical_not(wait))(lambda link=link, part=part: start_rows(link, part))
 
     for side, is_self in ((0, self_a), (1, self_b)):
-        pl.when(is_self)(lambda side=side: start_all(self_corner(side)))
+        pl.when(is_self)(lambda side=side: self_corner(side).start())
 
     for link in (W, E, N, NA, NB, S, SA, SB):
 
@@ -336,20 +339,17 @@
     received(raw_high + made_high)
     for side, is_self in ((0, self_a), (1, self_b)):
 
-        @pl.when(is_self)
-        def _(side=side):
-            for copy in self_corner(side):
-                copy.wait()
+        pl.when(is_self)(lambda side=side: self_corner(side).wait())
 
         @pl.when(jnp.logical_not(is_self))
         def _(side=side):
-            received(corners_high[side])
-            sent(corners_low[side])
+            corners_high[side].wait_recv()
+            corners_low[side].wait_send()
 
     @pl.when(has_south)
     def _():
-        received(raw_low + made_low + corners_low[0] + corners_low[1])
-        sent(raw_high + made_high + corners_high[0] + corners_high[1])
+        received(raw_low + made_low + corners_low)
+        sent(raw_high + made_high + corners_high)
 
     sent(raw_low + made_low)
     sent(strips_lon)
@@ -362,8 +362,8 @@
         partial(gather_kernel, lon_count, lat_count),
         out_shape=(
             jax.ShapeDtypeStruct((NFLD, EXT, COLS), f32),
-            jax.ShapeDtypeStruct((2, 2, WIDE, COLS), f32),
-            jax.ShapeDtypeStruct((2, 2 * (PAD - NEAR), COLS), f32),
+            jax.ShapeDtypeStruct((2, 2, ROWS, COLS), f32),
+            jax.ShapeDtypeStruct((2, 2, 3, TILE, COLS), f32),
         ),
         in_specs=[pl.BlockSpec(memory_space=pltpu.HBM)] * 6,
         out_specs=(anywhere, anywhere, anywhere),
@@ -375,11 +375,11 @@
             pltpu.VMEM((2, ROWS, COLS), f32),
             pltpu.VMEM((4, ROWS, COLS), f32),
             pltpu.VMEM((2, 2, ROWS, COLS), f32),
-            pltpu.VMEM((2, ROWS, COLS), f32),
+            pltpu.VMEM((2, 2, 3, TILE, COLS), f32),
             pltpu.SemaphoreType.DMA((6,)),
-            pltpu.SemaphoreType.DMA((22,)),
-            pltpu.SemaphoreType.DMA((22,)),
-            pltpu.SemaphoreType.DMA((4,)),
+            pltpu.SemaphoreType.DMA((16,)),
+            pltpu.SemaphoreType.DMA((16,)),
+            pltpu.SemaphoreType.DMA((2,)),
             pltpu.SemaphoreType.REGULAR((8,)),
         ],
         compiler_params=pltpu.CompilerParams(
@@ -388,13 +388,16 @@
     )(*operands)
 
 
-TILE = 8
-
-
 def tiles_for(reach):
     low = (PAD - reach) // TILE
     high = -(-(PAD + ROWS + reach) // TILE)
     return range(low * TILE, high * TILE, TILE)
+
+
+def working(raw):
+    s1, s2, s12, strength, mask = raw
+    cover = mask * (1.0 / 1.5)
+    return [0.125 * (s1 + s2), 0.125 * (s1 - s2), 0.25 * s12, (1.0 / 16.0) * cover * strength, cover]
 
 
 def flip_tile(value):
@@ -414,7 +417,7 @@
     cot,
     ext,
     land,
-    far,
+    corners,
     final_vel,
     vel_grad,
     sig_grad,
@@ -435,48 +438,53 @@
     last_lane = lane == COLS - 1
 
     wind_f32 = wind[...].astype(jnp.float32)
+    def store(plane, rows, q):
+        q[2:7] = working(q[2:7])
+        for field, value in enumerate(q):
+            fld[field, plane, rows] = value
+
     for r in range(0, EXT, TILE):
         rows = pl.ds(r, TILE)
-        side = []
-        for field in range(NFLD):
-            if PAD - NEAR <= r < PAD + ROWS + NEAR:
-                plane, to, width = slot_of(field)
-                near = pl.ds(r - PAD + NEAR, TILE)
-                side.append(unstrip(land[0, plane, near], land[1, plane, near], to, width))
-            else:
-                to, width = far_slot_of(field)
-                beyond = pl.ds(r if r < PAD else r - ROWS - 2 * NEAR, TILE)
-                side.append(unstrip(far[0, beyond], far[1, beyond], to, width))
         if PAD <= r < PAD + ROWS:
             mine = pl.ds(r - PAD, TILE)
-            main = [vel[0, mine], vel[1, mine], sig[0, mine], sig[1, mine], sig[2, mine], strength[mine]]
-            main += [mask[mine].astype(jnp.float32), wind_f32[0, r - PAD : r - PAD + TILE], wind_f32[1, r - PAD : r - PAD + TILE], cot[0, mine], cot[1, mine]]
+            at = slice(r - PAD, r - PAD + TILE)
+            q = [vel[0, mine], vel[1, mine], sig[0, mine], sig[1, mine], sig[2, mine], strength[mine]]
+            store(0, rows, q + [mask[mine].astype(jnp.float32), wind_f32[0, at], wind_f32[1, at], cot[0, mine], cot[1, mine]])
+            q = []
+            for field in range(NFLD):
+                plane, to, width = slot_of(field)
+                q.append(unstrip(land[0, plane, mine], land[1, plane, mine], to, width))
+            store(1, rows, q)
         else:
-            main = [ext[field, rows] for field in range(NFLD)]
-        if r < PAD:
-            main = [jnp.where(bottom, 0.0, x) for x in main]
-            side = [jnp.where(bottom, 0.0, x) for x in side]
-        for p, q in enumerate((main, side)):
-            cover = q[6] * (1.0 / 1.5)
-            q[2:7] = [
-                0.125 * (q[2] + q[3]),
-                0.125 * (q[2] - q[3]),
-                0.25 * q[4],
-                (1.0 / 16.0) * cover * q[5],
-                cover,
-            ]
-            for field in range(NFLD):
-                fld[field, p, rows] = q[field]
+            q = [ext[field, rows] for field in range(NFLD)]
+            store(0, rows, [jnp.where(bottom, 0.0, x) for x in q] if r < PAD else q)
+
+    def place_corners(end, turned):
+        for group in range(3):
+            q = [None] * NFLD
+            for plane, slots in enumerate(corner_slots()):
+                for of, field, to, width in slots:
+                    if of == group:
+                        q[field] = unstrip(corners[0, end, plane], corners[1, end, plane], to, width)
+            q = [jnp.zeros(shape, jnp.float32) if x is None else x for x in q]
+            if end == 1:
+                q = [jnp.where(bottom, 0.0, x) for x in q]
+            if turned:
+                q = [-flip_tile(x) if field in ODD_FIELDS else flip_tile(x) for field, x in enumerate(q)]
+            row = PAD + ROWS + GROUP * group if end == 0 else PAD - TILE - GROUP * group
+            store(1, pl.ds(row, TILE), q)
+
+    place_corners(1, False)
+    pl.when(jnp.logical_not(top))(lambda: place_corners(0, False))
+    pl.when(top)(lambda: place_corners(0, True))
 
     @pl.when(top)
     def _():
         for field in range(NFLD):
-            for plane in range(2):
-                old = [fld[field, plane, pl.ds(PAD + ROWS + t * TILE, TILE)] for t in range(3)]
-                order = (2, 1, 0) if plane == 0 else (0, 2, 1)
-                for t in range(3):
-                    new = flip_tile(old[order[t]])
-                    fld[field, plane, pl.ds(PAD + ROWS + t * TILE, TILE)] = -new if field in ODD_FIELDS else new
+            old = [fld[field, 0, pl.ds(PAD + ROWS + t * TILE, TILE)] for t in range(3)]
+            for t in range(3):
+                new = flip_tile(old[2 - t])
+                fld[field, 0, pl.ds(PAD + ROWS + t * TILE, TILE)] = -new if field in ODD_FIELDS else new
 
     for r in range(0, EXT, TILE):
         rows = pl.ds(r, TILE)

time: 31.3 us -> 30.5 us (0.974)
  Pallas kernels: 29.4 us -> 28.9 us
    pallas_call x1, Pallas kernels: 26.1 us -> 25.5 us  [gather_halos(): pl.pallas_call(partial(gather_kernel, lon_count, lat_count), out_shape=(j...]
where the time goes in v5:
time: 30.5 us; the launch traced here: 30.3 us
  Pallas kernels  28.9 us (95%)
  between operations  1.38 us (5%)
    pallas_call x1, Pallas kernels, gather_halos(): pl.pallas_call(partial(gather_kernel, lon_count, lat_count), out_shape=(j...  25.5 us
    pallas_call x1, Pallas kernels, evp_and_adjoint(): pl.pallas_call(partial(evp_kernel, lat_count), out_shape=(jax.ShapeDtypeS...  3.35 us

profile of v5, /device:TPU:6, one launch (start us, length us, event | category | flops | bytes accessed | tf_op | source)
XLA Modules:
  0.0 30.3 jit_solution(5965153134546588995)
XLA Ops:
  1.3 0.0 copy-start
  1.3 0.0 copy-start.1
  1.3 0.0 copy-start.2
  1.3 0.0 copy-start.3
  1.3 0.0 copy-start.4
  1.3 0.0 copy-start.5
  1.3 25.5 %shard_map.94 = (f32[11,96,128]{2,1,0:T(8,128)S(1)}, f32[2,2,48,128]{3,2,1,0:T(8,128)S(1)}, f32[2,2,3,8,128]{4,3,2,1,0:T(8,128)S(1)}) custom-call(f32[2,48,128]{2,1,0:T(8,128)} %vel.3, f32[3,48,128]{2,1,0:T(8,128)} %sig.3, f32[48,128]{1,0:T(8,128)} %strength.3, bf16[2,48,128]{2,1,0:T(8,128)(2,1)} %wind.3, s32[48,128]{1,0:T(8,128)} %mask.3, f32[2,48,128]{2,1,0:T(8,128)} %cot.3), custom_call_target="tpu_custom_call" | custom-call | tf_op jit(solution)/shard_map/pallas_call | solution.py:361
  26.9 0.0 copy-done
  26.9 0.0 copy-done.1
  26.9 0.0 copy-done.2
  26.9 0.0 copy-done.3
  26.9 0.0 copy-done.4
  26.9 0.0 copy-done.5
  26.9 3.3 %shard_map.95 = (f32[2,48,128]{2,1,0:T(8,128)}, f32[2,48,128]{2,1,0:T(8,128)}, f32[3,48,128]{2,1,0:T(8,128)}) custom-call(s32[1]{0:T(128)S(6)} %copy.10.start, f32[2,48,128]{2,1,0:T(8,128)S(1)} %copy-done.1, f32[3,48,128]{2,1,0:T(8,128)S(1)} %copy-done, f32[48,128]{1,0:T(8,128)S(1)} %copy-done.3, bf16[2,48,128]{2,1,0:T(8,128)(2,1)S(1)} %copy-done.4, ...), custom_call_target="tpu_custom_call" | custom-call | tf_op jit(solution)/shard_map/pallas_call | solution.py:643
Async XLA Ops:
  1.3 25.6 %copy-start = (f32[3,48,128]{2,1,0:T(8,128)S(1)}, f32[3,48,128]{2,1,0:T(8,128)}, u32[]{:S(2)}) copy-start(f32[3,48,128]{2,1,0:T(8,128)} %sig.3) | copy-start | bytes 221188
  1.3 25.6 %copy-start.1 = (f32[2,48,128]{2,1,0:T(8,128)S(1)}, f32[2,48,128]{2,1,0:T(8,128)}, u32[]{:S(2)}) copy-start(f32[2,48,128]{2,1,0:T(8,128)} %vel.3) | copy-start | bytes 147460
  1.3 25.6 %copy-start.2 = (f32[2,48,128]{2,1,0:T(8,128)S(1)}, f32[2,48,128]{2,1,0:T(8,128)}, u32[]{:S(2)}) copy-start(f32[2,48,128]{2,1,0:T(8,128)} %cot.3) | copy-start | bytes 147460
  1.3 25.6 %copy-start.3 = (f32[48,128]{1,0:T(8,128)S(1)}, f32[48,128]{1,0:T(8,128)}, u32[]{:S(2)}) copy-start(f32[48,128]{1,0:T(8,128)} %strength.3) | copy-start | bytes 73732
  1.3 25.6 %copy-start.4 = (bf16[2,48,128]{2,1,0:T(8,128)(2,1)S(1)}, bf16[2,48,128]{2,1,0:T(8,128)(2,1)}, u32[]{:S(2)}) copy-start(bf16[2,48,128]{2,1,0:T(8,128)(2,1)} %wind.3) | copy-start | bytes 73732
  1.3 25.6 %copy-start.5 = (s32[48,128]{1,0:T(8,128)S(1)}, s32[48,128]{1,0:T(8,128)}, u32[]{:S(2)}) copy-start(s32[48,128]{1,0:T(8,128)} %mask.3) | copy-start | bytes 73732

commit v6 on v5

--- a/solution.py
+++ b/solution.py
@@ -96,7 +96,7 @@
     x = digit(lat, 4, 4)
     z_high = lat - 4 * x
     early_half = z_high < 2
-    base = jnp.where(early_half, 44 * z_high, 96 - 4 * z_high)
+    base = jnp.where(early_half, 44 * z_high, jnp.where(z_high == 2, 130, 84))
     step = jnp.where(early_half, 13, 4)
     return 1024 * (7 * x + 7 * y + base + step * z_low) + 32 * lat + lon
 
@@ -274,14 +274,19 @@
 
     count = sum(jnp.where(g, 1, 0) for g in greeted)
     pl.when(count > 0)(lambda: pl.semaphore_wait(barrier, count))
+    patient = top & (lon < lon_count // 2)
+    corners_first = inner & (lon == lon_count - 1)
+    for link in (N, S):
+        wait = corners_first | patient if link == N else corners_first
+        pl.when(greeted[link] & jnp.logical_not(corners_first))(lambda link=link: start_rows(link, 0))
+        pl.when(greeted[link] & jnp.logical_not(wait))(lambda link=link: start_rows(link, 1))
+
     for link in range(8):
 
         @pl.when(answers[link])
         def _(link=link):
             pl.semaphore_signal(ready.at[reverse[link]], inc=1, device_id=partner[link], device_id_type=MESH)
 
-    for link in (N, S):
-        pl.when(greeted[link])(lambda link=link: start_rows(link, 0))
 
     for copy in loads:
         copy.wait()
@@ -301,18 +306,18 @@
                 parts = [block[field][pl.ds(corner_rows(end, group), TILE)] for group, field, _, _ in slots]
                 corner_pack[side, end, plane] = strips(parts, [slot[2:] for slot in slots], side, (TILE, COLS))
 
-    for link in (NA, NB, SA, SB, W, E):
+    for link in (NB, SB, NA, SA, W, E):
         pl.when(greeted[link])(lambda link=link: start_strips(link))
-    patient = top & (lon < lon_count // 2)
-    for part in (1, 2):
-        for link in (N, S):
-            wait = patient if link == N else jnp.logical_not(always)
-            pl.when(greeted[link] & jnp.logical_not(wait))(lambda link=link, part=part: start_rows(link, part))
+    for link in (N, S):
+        for part in (0, 1):
+            pl.when(greeted[link] & corners_first)(lambda link=link, part=part: start_rows(link, part))
+        wait = patient if link == N else jnp.logical_not(always)
+        pl.when(greeted[link] & jnp.logical_not(wait))(lambda link=link: start_rows(link, 2))
 
     for side, is_self in ((0, self_a), (1, self_b)):
         pl.when(is_self)(lambda side=side: self_corner(side).start())
 
-    for link in (W, E, N, NA, NB, S, SA, SB):
+    for link in (W, E, N, S, NB, SB, NA, SA):
 
         @pl.when(awaits[link])
         def _(link=link):

time: 30.5 us -> 29.7 us (0.974)
  Pallas kernels: 28.9 us -> 27.9 us
    pallas_call x1, Pallas kernels: 25.5 us -> 24.6 us  [gather_halos(): pl.pallas_call(partial(gather_kernel, lon_count, lat_count), out_shape=(j...]
where the time goes in v6:
time: 29.7 us; the launch traced here: 29.3 us
  Pallas kernels  27.9 us (94%)
  between operations  1.38 us (5%)
    pallas_call x1, Pallas kernels, gather_halos(): pl.pallas_call(partial(gather_kernel, lon_count, lat_count), out_shape=(j...  24.6 us
    pallas_call x1, Pallas kernels, evp_and_adjoint(): pl.pallas_call(partial(evp_kernel, lat_count), out_shape=(jax.ShapeDtypeS...  3.35 us

profile of v6, /device:TPU:6, one launch (start us, length us, event | category | flops | bytes accessed | tf_op | source)
XLA Modules:
  0.0 29.3 jit_solution(14251831500760342636)
XLA Ops:
  1.3 0.0 copy-start
  1.3 0.0 copy-start.1
  1.3 0.0 copy-start.2
  1.3 0.0 copy-start.3
  1.3 0.0 copy-start.4
  1.3 0.0 copy-start.5
  1.3 24.6 %shard_map.94 = (f32[11,96,128]{2,1,0:T(8,128)S(1)}, f32[2,2,48,128]{3,2,1,0:T(8,128)S(1)}, f32[2,2,3,8,128]{4,3,2,1,0:T(8,128)S(1)}) custom-call(f32[2,48,128]{2,1,0:T(8,128)} %vel.3, f32[3,48,128]{2,1,0:T(8,128)} %sig.3, f32[48,128]{1,0:T(8,128)} %strength.3, bf16[2,48,128]{2,1,0:T(8,128)(2,1)} %wind.3, s32[48,128]{1,0:T(8,128)} %mask.3, f32[2,48,128]{2,1,0:T(8,128)} %cot.3), custom_call_target="tpu_custom_call" | custom-call | tf_op jit(solution)/shard_map/pallas_call | solution.py:366
  25.9 0.0 copy-done
  25.9 0.0 copy-done.1
  26.0 0.0 copy-done.2
  26.0 0.0 copy-done.3
  26.0 0.0 copy-done.4
  26.0 0.0 copy-done.5
  26.0 3.3 %shard_map.95 = (f32[2,48,128]{2,1,0:T(8,128)}, f32[2,48,128]{2,1,0:T(8,128)}, f32[3,48,128]{2,1,0:T(8,128)}) custom-call(s32[1]{0:T(128)S(6)} %copy.10.start, f32[2,48,128]{2,1,0:T(8,128)S(1)} %copy-done.1, f32[3,48,128]{2,1,0:T(8,128)S(1)} %copy-done, f32[48,128]{1,0:T(8,128)S(1)} %copy-done.3, bf16[2,48,128]{2,1,0:T(8,128)(2,1)S(1)} %copy-done.4, ...), custom_call_target="tpu_custom_call" | custom-call | tf_op jit(solution)/shard_map/pallas_call | solution.py:648
Async XLA Ops:
  1.3 24.7 %copy-start = (f32[3,48,128]{2,1,0:T(8,128)S(1)}, f32[3,48,128]{2,1,0:T(8,128)}, u32[]{:S(2)}) copy-start(f32[3,48,128]{2,1,0:T(8,128)} %sig.3) | copy-start | bytes 221188
  1.3 24.7 %copy-start.1 = (f32[2,48,128]{2,1,0:T(8,128)S(1)}, f32[2,48,128]{2,1,0:T(8,128)}, u32[]{:S(2)}) copy-start(f32[2,48,128]{2,1,0:T(8,128)} %vel.3) | copy-start | bytes 147460
  1.3 24.7 %copy-start.2 = (f32[2,48,128]{2,1,0:T(8,128)S(1)}, f32[2,48,128]{2,1,0:T(8,128)}, u32[]{:S(2)}) copy-start(f32[2,48,128]{2,1,0:T(8,128)} %cot.3) | copy-start | bytes 147460
  1.3 24.7 %copy-start.3 = (f32[48,128]{1,0:T(8,128)S(1)}, f32[48,128]{1,0:T(8,128)}, u32[]{:S(2)}) copy-start(f32[48,128]{1,0:T(8,128)} %strength.3) | copy-start | bytes 73732
  1.3 24.7 %copy-start.4 = (bf16[2,48,128]{2,1,0:T(8,128)(2,1)S(1)}, bf16[2,48,128]{2,1,0:T(8,128)(2,1)}, u32[]{:S(2)}) copy-start(bf16[2,48,128]{2,1,0:T(8,128)(2,1)} %wind.3) | copy-start | bytes 73732
  1.3 24.7 %copy-start.5 = (s32[48,128]{1,0:T(8,128)S(1)}, s32[48,128]{1,0:T(8,128)}, u32[]{:S(2)}) copy-start(s32[48,128]{1,0:T(8,128)} %mask.3) | copy-start | bytes 73732

commit v7 on v6

--- a/solution.py
+++ b/solution.py
@@ -274,19 +274,19 @@
 
     count = sum(jnp.where(g, 1, 0) for g in greeted)
     pl.when(count > 0)(lambda: pl.semaphore_wait(barrier, count))
+    for link in (N, S, NB, SB, NA, SA, W, E):
+
+        @pl.when(answers[link])
+        def _(link=link):
+            pl.semaphore_signal(ready.at[reverse[link]], inc=1, device_id=partner[link], device_id_type=MESH)
+
+
     patient = top & (lon < lon_count // 2)
     corners_first = inner & (lon == lon_count - 1)
     for link in (N, S):
         wait = corners_first | patient if link == N else corners_first
         pl.when(greeted[link] & jnp.logical_not(corners_first))(lambda link=link: start_rows(link, 0))
         pl.when(greeted[link] & jnp.logical_not(wait))(lambda link=link: start_rows(link, 1))
-
-    for link in range(8):
-
-        @pl.when(answers[link])
-        def _(link=link):
-            pl.semaphore_signal(ready.at[reverse[link]], inc=1, device_id=partner[link], device_id_type=MESH)
-
 
     for copy in loads:
         copy.wait()

time: 29.7 us -> 29.7 us (level)
  no operation moved by 1% of the time
where the time goes in v7:
time: 29.7 us; the launch traced here: 29.3 us
  Pallas kernels  27.9 us (94%)
  between operations  1.38 us (5%)
    pallas_call x1, Pallas kernels, gather_halos(): pl.pallas_call(partial(gather_kernel, lon_count, lat_count), out_shape=(j...  24.6 us
    pallas_call x1, Pallas kernels, evp_and_adjoint(): pl.pallas_call(partial(evp_kernel, lat_count), out_shape=(jax.ShapeDtypeS...  3.35 us

profile of v7, /device:TPU:6, one launch (start us, length us, event | category | flops | bytes accessed | tf_op | source)
XLA Modules:
  0.0 29.3 jit_solution(1133620908331283632)
XLA Ops:
  1.3 0.0 copy-start
  1.3 0.0 copy-start.1
  1.3 0.0 copy-start.2
  1.3 0.0 copy-start.3
  1.3 0.0 copy-start.4
  1.3 0.0 copy-start.5
  1.3 24.6 %shard_map.94 = (f32[11,96,128]{2,1,0:T(8,128)S(1)}, f32[2,2,48,128]{3,2,1,0:T(8,128)S(1)}, f32[2,2,3,8,128]{4,3,2,1,0:T(8,128)S(1)}) custom-call(f32[2,48,128]{2,1,0:T(8,128)} %vel.3, f32[3,48,128]{2,1,0:T(8,128)} %sig.3, f32[48,128]{1,0:T(8,128)} %strength.3, bf16[2,48,128]{2,1,0:T(8,128)(2,1)} %wind.3, s32[48,128]{1,0:T(8,128)} %mask.3, f32[2,48,128]{2,1,0:T(8,128)} %cot.3), custom_call_target="tpu_custom_call" | custom-call | tf_op jit(solution)/shard_map/pallas_call | solution.py:366
  25.9 0.0 copy-done
  25.9 0.0 copy-done.1
  26.0 0.0 copy-done.2
  26.0 0.0 copy-done.3
  26.0 0.0 copy-done.4
  26.0 0.0 copy-done.5
  26.0 3.3 %shard_map.95 = (f32[2,48,128]{2,1,0:T(8,128)}, f32[2,48,128]{2,1,0:T(8,128)}, f32[3,48,128]{2,1,0:T(8,128)}) custom-call(s32[1]{0:T(128)S(6)} %copy.10.start, f32[2,48,128]{2,1,0:T(8,128)S(1)} %copy-done.1, f32[3,48,128]{2,1,0:T(8,128)S(1)} %copy-done, f32[48,128]{1,0:T(8,128)S(1)} %copy-done.3, bf16[2,48,128]{2,1,0:T(8,128)(2,1)S(1)} %copy-done.4, ...), custom_call_target="tpu_custom_call" | custom-call | tf_op jit(solution)/shard_map/pallas_call | solution.py:648
Async XLA Ops:
  1.3 24.7 %copy-start = (f32[3,48,128]{2,1,0:T(8,128)S(1)}, f32[3,48,128]{2,1,0:T(8,128)}, u32[]{:S(2)}) copy-start(f32[3,48,128]{2,1,0:T(8,128)} %sig.3) | copy-start | bytes 221188
  1.3 24.7 %copy-start.1 = (f32[2,48,128]{2,1,0:T(8,128)S(1)}, f32[2,48,128]{2,1,0:T(8,128)}, u32[]{:S(2)}) copy-start(f32[2,48,128]{2,1,0:T(8,128)} %vel.3) | copy-start | bytes 147460
  1.3 24.7 %copy-start.2 = (f32[2,48,128]{2,1,0:T(8,128)S(1)}, f32[2,48,128]{2,1,0:T(8,128)}, u32[]{:S(2)}) copy-start(f32[2,48,128]{2,1,0:T(8,128)} %cot.3) | copy-start | bytes 147460
  1.3 24.7 %copy-start.3 = (f32[48,128]{1,0:T(8,128)S(1)}, f32[48,128]{1,0:T(8,128)}, u32[]{:S(2)}) copy-start(f32[48,128]{1,0:T(8,128)} %strength.3) | copy-start | bytes 73732
  1.3 24.7 %copy-start.4 = (bf16[2,48,128]{2,1,0:T(8,128)(2,1)S(1)}, bf16[2,48,128]{2,1,0:T(8,128)(2,1)}, u32[]{:S(2)}) copy-start(bf16[2,48,128]{2,1,0:T(8,128)(2,1)} %wind.3) | copy-start | bytes 73732
  1.3 24.7 %copy-start.5 = (s32[48,128]{1,0:T(8,128)S(1)}, s32[48,128]{1,0:T(8,128)}, u32[]{:S(2)}) copy-start(s32[48,128]{1,0:T(8,128)} %mask.3) | copy-start | bytes 73732
